TPU v7x, 32 devices: a whole 2x2x4 slice. The times are simulated.
32 devices in a mesh: vel: 8 (over y, x, core), gx: 4 (over z).
Axes of the slice: x: 2, y: 2, z: 4, core: 2. Of those that a mesh axis runs over, the one named last changes fastest.
Arguments:
- distribution: float32 [4096, 8192], P('vel', 'gx'), as said below
- wall_mask: int32 [16, 512], replicated, may hold values 0 or 1
- boundary_kind: int32 [2, 512], replicated, may hold values from 0 to 1
- inflow: float32 [4096], P('vel'), may hold values from 0.5 to 3
Outputs:
- evolved: float32 [4096, 8192], P('vel', 'gx')
Inputs may be any that keep to these rules, and one draw needn't show every extreme that they name: `distribution`: every entry is positive. `wall_mask`: 1 marks a solid cell. `boundary_kind`: 0 is an outflow face, 1 an inflow face.
All inputs are finite; a program needn't handle non-finite values.
Results may differ from a plain program's by a relative error of at most 0.0003.
Values sent between devices are 32-bit elements; how exact they have to be, the bound alone decides.
A program may use at most 128 MiB of HBM per device.

v0:
```python
import jax
import jax.numpy as jnp
from jax import lax
from jax.sharding import PartitionSpec as P

VS = 16
NY = 16
NZ = 32
STEPS = 3


vel_limit = 4.5
time_step = 0.075
relax_rate = 0.6
viscous_thermal_ratio = 0.6666667


def passed_along(array, axis, by):
    peers = lax.axis_size(axis)
    pairs = [(i, i + by) for i in range(peers) if 0 <= i + by < peers]
    return lax.ppermute(array, axis, pairs)


def velocity_rows(lattice_lines):
    square = VS * VS
    half = square // 2
    across = lattice_lines // square
    rest = lattice_lines % square
    upper = rest // half
    inner = rest % half
    along = jnp.where(upper == 1, VS // 2 + inner // VS, VS // 2 - 1 - inner // VS)
    depth = inner % VS
    spacing = 2.0 * vel_limit / VS

    def coord(index):
        return -vel_limit + (index.astype(jnp.float32) + 0.5) * spacing

    return (coord(along), coord(across), coord(depth))


def poly_basis(speed_x, speed_y, speed_z):
    energy = speed_x * speed_x + speed_y * speed_y + speed_z * speed_z
    return jnp.stack(
        [
            jnp.ones_like(speed_x),
            speed_x,
            speed_y,
            speed_z,
            speed_x * speed_x,
            speed_y * speed_y,
            speed_z * speed_z,
            speed_x * speed_y,
            speed_x * speed_z,
            speed_y * speed_z,
            energy * speed_x,
            energy * speed_y,
            energy * speed_z,
        ],
        axis=1,
    )


def exp_basis(speed_x, speed_y, speed_z):
    energy = speed_x * speed_x + speed_y * speed_y + speed_z * speed_z
    return jnp.stack([jnp.ones_like(speed_x), speed_x, speed_y, speed_z, energy], axis=1)


def shakhov_coefficients(moments):
    particle_concentration = moments[0]
    mean_drift_first = moments[1] / particle_concentration
    mean_drift_second = moments[2] / particle_concentration
    mean_drift_third_dir = moments[3] / particle_concentration
    second = moments[4:10]
    motion_work_content = (
        mean_drift_first * mean_drift_first
        + mean_drift_second * mean_drift_second
        + mean_drift_third_dir * mean_drift_third_dir
    )
    pressure_diagonal_sum = second[0] + second[1] + second[2]
    thermal_level = (pressure_diagonal_sum / particle_concentration - motion_work_content) / 3.0
    press_x = (
        second[0] * mean_drift_first
        + second[3] * mean_drift_second
        + second[4] * mean_drift_third_dir
    )
    press_y = (
        second[3] * mean_drift_first
        + second[1] * mean_drift_second
        + second[5] * mean_drift_third_dir
    )
    press_z = (
        second[4] * mean_drift_first
        + second[5] * mean_drift_second
        + second[2] * mean_drift_third_dir
    )
    heat_x = 0.5 * (
        moments[10]
        - 2.0 * press_x
        - mean_drift_first * pressure_diagonal_sum
        + 2.0 * particle_concentration * motion_work_content * mean_drift_first
    )
    heat_y = 0.5 * (
        moments[11]
        - 2.0 * press_y
        - mean_drift_second * pressure_diagonal_sum
        + 2.0 * particle_concentration * motion_work_content * mean_drift_second
    )
    heat_z = 0.5 * (
        moments[12]
        - 2.0 * press_z
        - mean_drift_third_dir * pressure_diagonal_sum
        + 2.0 * particle_concentration * motion_work_content * mean_drift_third_dir
    )
    heat_diffusivity_coef = (1.0 - viscous_thermal_ratio) / (
        5.0 * particle_concentration * thermal_level * thermal_level
    )
    quadrature_scale = heat_diffusivity_coef / thermal_level
    mixed = mean_drift_first * heat_x + mean_drift_second * heat_y + mean_drift_third_dir * heat_z
    foremost_dimension = (
        jnp.log(particle_concentration)
        - 1.5 * jnp.log(2.0 * jnp.pi * thermal_level)
        - motion_work_content / (2.0 * thermal_level)
    )
    lattice_lines = [
        foremost_dimension,
        mean_drift_first / thermal_level,
        mean_drift_second / thermal_level,
        mean_drift_third_dir / thermal_level,
        -0.5 / thermal_level,
        1.0 - quadrature_scale * mixed * motion_work_content + 5.0 * heat_diffusivity_coef * mixed,
        quadrature_scale * (heat_x * motion_work_content + 2.0 * mixed * mean_drift_first)
        - 5.0 * heat_diffusivity_coef * heat_x,
        quadrature_scale * (heat_y * motion_work_content + 2.0 * mixed * mean_drift_second)
        - 5.0 * heat_diffusivity_coef * heat_y,
        quadrature_scale * (heat_z * motion_work_content + 2.0 * mixed * mean_drift_third_dir)
        - 5.0 * heat_diffusivity_coef * heat_z,
        -2.0 * quadrature_scale * heat_x * mean_drift_first - quadrature_scale * mixed,
        -2.0 * quadrature_scale * heat_y * mean_drift_second - quadrature_scale * mixed,
        -2.0 * quadrature_scale * heat_z * mean_drift_third_dir - quadrature_scale * mixed,
        -2.0 * quadrature_scale * (heat_x * mean_drift_second + heat_y * mean_drift_first),
        -2.0 * quadrature_scale * (heat_x * mean_drift_third_dir + heat_z * mean_drift_first),
        -2.0 * quadrature_scale * (heat_y * mean_drift_third_dir + heat_z * mean_drift_second),
        quadrature_scale * heat_x,
        quadrature_scale * heat_y,
        quadrature_scale * heat_z,
    ]
    return jnp.stack(lattice_lines, axis=0)


def relax(moved, coefficients, expo_rows, poly_rows):
    power = jnp.dot(expo_rows, coefficients[0:5], precision=lax.Precision.HIGHEST)
    shape = jnp.dot(poly_rows, coefficients[5:18], precision=lax.Precision.HIGHEST)
    return moved + relax_rate * (jnp.exp(power) * shape - moved)


def per_device(distribution, wall_mask, boundary_kind, inflow):
    rows_dev = distribution.shape[0]
    cells_dev = distribution.shape[1]
    section = wall_mask.shape[1]
    depth = cells_dev // section
    half = VS * VS // 2
    blocks = rows_dev // (2 * half)
    position = lax.axis_index("gx")
    at_low = position == 0
    at_high = position == lax.axis_size("gx") - 1
    lattice_lines = lax.axis_index("vel") * rows_dev + jnp.arange(rows_dev, dtype=jnp.int32)
    speed_x, speed_y, speed_z = velocity_rows(lattice_lines)
    poly = poly_basis(speed_x, speed_y, speed_z)
    expo = exp_basis(speed_x, speed_y, speed_z)
    weight = (2.0 * vel_limit / VS) ** 3
    openness = (1 - wall_mask).astype(jnp.float32)
    open_pad = jnp.pad(openness, ((1, 1), (0, 0)), constant_values=1.0)
    local_open = lax.dynamic_slice_in_dim(open_pad, position * depth, depth + 2, 0)
    inner_open = local_open[1:-1]
    low_in = boundary_kind[0] == 1
    high_in = boundary_kind[1] == 1
    entering = inflow.reshape(blocks, 2, half)
    lanes = jnp.arange(section, dtype=jnp.int32)
    open_y = (
        inner_open * jnp.roll(inner_open, -NZ, axis=1) * (lanes // NZ < NY - 1).astype(jnp.float32)
    )
    open_z = (
        inner_open * jnp.roll(inner_open, -1, axis=1) * (lanes % NZ < NZ - 1).astype(jnp.float32)
    )
    open_x = local_open[:-1] * local_open[1:]

    def send_rims(state3):
        view = state3.reshape(blocks, 2, half, depth, section)
        from_left = passed_along(view[:, 1, :, depth - 1], "gx", 1)
        from_right = passed_along(view[:, 0, :, 0], "gx", -1)
        return (from_left, from_right)

    state = distribution.reshape(rows_dev, depth, section)
    from_left, from_right = send_rims(state)
    for step in range(STEPS):
        last = step + 1 == STEPS
        transport_view = state.reshape(blocks, 2, half, depth, section)
        low_value = jnp.where(
            low_in[None, None, :], entering[:, 1, :, None], transport_view[:, 1, :, 0]
        )
        ghost_upper = jnp.where(at_low, low_value, from_left)
        high_value = jnp.where(
            high_in[None, None, :], entering[:, 0, :, None], transport_view[:, 0, :, depth - 1]
        )
        ghost_lower = jnp.where(at_high, high_value, from_right)
        zeros = jnp.zeros_like(ghost_upper)
        left = jnp.stack([zeros, ghost_upper], axis=1).reshape(rows_dev, 1, section)
        right = jnp.stack([ghost_lower, zeros], axis=1).reshape(rows_dev, 1, section)
        extended = jnp.concatenate([left, state, right], axis=1)
        speed = speed_x[:, None, None]
        upwind = jnp.where(speed > 0, extended[:, :-1], extended[:, 1:])
        flux = speed * upwind * open_x
        change = flux[:, 1:] - flux[:, :-1]
        speed = speed_y[:, None, None]
        flux = speed * jnp.where(speed > 0, state, jnp.roll(state, -NZ, axis=2)) * open_y
        change = change + (flux - jnp.roll(flux, NZ, axis=2))
        speed = speed_z[:, None, None]
        flux = speed * jnp.where(speed > 0, state, jnp.roll(state, -1, axis=2)) * open_z
        change = change + (flux - jnp.roll(flux, 1, axis=2))
        moved = state - time_step * change
        moved2 = moved.reshape(rows_dev, cells_dev)
        partial_value = weight * jnp.dot(poly.T, moved2, precision=lax.Precision.HIGHEST)
        owned = lax.psum_scatter(partial_value, "vel", scatter_dimension=1, tiled=True)
        coefficients = lax.all_gather(shakhov_coefficients(owned), "vel", axis=1, tiled=True)
        state = relax(moved2, coefficients, expo, poly).reshape(rows_dev, depth, section)
        if not last:
            from_left, from_right = send_rims(state)
    return state.reshape(rows_dev, cells_dev)


def solution(mesh):
    placed = (P("vel", "gx"), P(), P(), P("vel"))
    return jax.shard_map(
        per_device, mesh=mesh, in_specs=placed, out_specs=P("vel", "gx"), check_vma=False
    )
```

profile of v0, /device:TPU:17, one launch (start us, length us, event | category | flops | bytes accessed | tf_op | source)
XLA Modules:
  0.0 398.7 jit_solution(8017287569526428337)
XLA Ops:
  6.5 6.0 %reshape_reshape.12 = f32[2,2,128,4,512]{4,3,2,1,0:T(4,128)} reshape(f32[512,2048]{1,0:T(8,128)} %param.4) | data formatting | bytes 8388608 | tf_op jit(solution)/shard_map/reshape;reshape | solution.py:197
  12.6 6.2 %fusion.150 = (f32[2,1,128,1,512]{4,3,2,1,0:T(1,128)S(1)}, f32[2,1,128,1,512]{4,3,2,1,0:T(1,128)}, f32[2,1,128,1,512]{4,3,2,1,0:T(1,128)S(1)}, f32[2,1,128,1,512]{4,3,2,1,0:T(1,128)S(1)}) fusion(f32[2,2,128,4,512]{4,3,2,1,0:T(4,128)} %reshape_reshape.12), kind=kLoop, calls=%fused_computation.333 | loop fusion | bytes 4194304 | tf_op jit(solution)/shard_map/slice | solution.py:203
  29.9 6.0 %reshape.490 = f32[512,4,512]{2,1,0:T(4,128)} reshape(f32[512,2048]{1,0:T(8,128)} %param.4) | data formatting | bytes 8388608 | tf_op jit(solution)/shard_map/reshape | solution.py:193
  35.9 6.6 %slice.475 = f32[512,4,511]{2,1,0:T(4,128)} slice(f32[512,4,512]{2,1,0:T(4,128)} %reshape.490), slice={[0:512], [0:4], [1:512]} | slice | bytes 8372224 | tf_op jit(solution)/shard_map/jit(_roll_static)/slice | solution.py:218
  47.0 12.3 %fusion.21 = (f32[512,4,512]{2,1,0:T(4,128)}, f32[512,4,512]{2,1,0:T(4,128)}) fusion(f32[512,4,512]{2,1,0:T(4,128)} %reshape.490, f32[512,4,1]{2,1,0:T(4,128)S(1)} %slice-done, f32[512,4,511]{2,1,0:T(4,128)} %slice.475, f32[4,512]{1,0:T(4,128)S(1)} %get-tuple-element.79, f32[512]{0:T(512)S(1)} %get-tuple-element.129, ...), kind=kLoop, calls=%fused_computation.30 | loop fusion | flops 8388608 | bytes 20993024 | tf_op jit(solution)/shard_map/mul | solution.py:218
  75.5 8.6 %fusion.17 = f32[512,4,512]{2,1,0:T(4,128)} fusion(f32[512,4,512]{2,1,0:T(4,128)S(1)} %copy-done.1, f32[512,5,512]{2,1,0:T(8,128)S(1)} %fusion.1, f32[512,4,512]{2,1,0:T(4,128)S(1)} %copy-done.7, f32[512,4,480]{2,1,0:T(4,128)S(1)} %bitcast.124, f32[512,4,32]{2,1,0:T(4,128)} %slice.473, f32[512,4,512]{2,1,0:T(4,128)S(1)} %copy-done.6, ...), kind=kLoop, calls=%fused_computation.23 | loop fusion | flops 9437184 | bytes 33554432 | tf_op jit(solution)/shard_map/sub | solution.py:220
  93.2 34.2 %reduce-scatter.4.cloned.1.call-done = f32[13,256]{1,0:T(8,128)} async-done(((f32[13,2048]{1,0:T(8,128)}), f32[13,256]{1,0:T(8,128)}) %reduce-scatter.4.cloned.1.call-update) | async-done | bytes 13328 | tf_op jit(solution)/shard_map/reduce_scatter | solution.py:223
  130.4 10.5 %all_gather.9 = f32[18,2048]{1,0:T(8,128)S(1)} all-gather(f32[18,256]{1,0:T(8,128)S(1)} %stack.40), channel_id=1, replica_groups=mesh['vel'=8,'gx'=4] {'vel'}, dimensions={1}, use_global_device_ids=true | all-gather | bytes 165888 | tf_op jit(solution)/shard_map/all_gather | solution.py:224
  144.3 6.3 %multiply_add_fusion.2 = f32[512,2048]{1,0:T(8,128)} fusion(f32[512,2048]{1,0:T(8,128)S(1)} %bitcast.130, f32[512,2048]{1,0:T(8,128)S(1)} %fusion.55, f32[512,13]{0,1:T(8,128)S(1)} %stack.39, f32[18,2048]{1,0:T(8,128)S(1)} %all_gather.9), kind=kOutput, calls=%fused_computation.50 | convolution fusion | flops 167772160 | bytes 12746752 | tf_op jit(solution)/shard_map/dot_general | solution.py:152
  150.6 6.1 %reshape.495 = f32[512,4,512]{2,1,0:T(4,128)} reshape(f32[512,2048]{1,0:T(8,128)} %multiply_add_fusion.2) | data formatting | bytes 8388608 | tf_op jit(solution)/shard_map/reshape | solution.py:225
  156.7 6.0 %reshape_reshape.13 = f32[2,2,128,4,512]{4,3,2,1,0:T(4,128)} reshape(f32[512,2048]{1,0:T(8,128)} %multiply_add_fusion.2) | data formatting | bytes 8388608 | tf_op jit(solution)/shard_map/reshape;reshape | solution.py:197
  176.9 9.5 %fusion.25 = (f32[512,4,512]{2,1,0:T(4,128)S(1)}, f32[512,4,512]{2,1,0:T(4,128)S(1)}) fusion(f32[512,4,512]{2,1,0:T(4,128)S(1)} %copy-done.5, f32[512,4,1]{2,1,0:T(4,128)S(1)} %slice-done.4, f32[512,4,511]{2,1,0:T(4,128)S(1)} %slice.504, f32[4,512]{1,0:T(4,128)S(1)} %copy-done.18, f32[512]{0:T(512)S(1)} %copy-done.22, pred[512]{0:T(512)(128)(4,1)S(1)} %copy-done.52, ...), kind=kLoop, calls=%fused_computation.38 | loop fusion | flops 8388608 | bytes 20993024 | tf_op jit(solution)/shard_map/mul | solution.py:218
  190.4 6.9 %fusion.3 = f32[512,5,512]{2,1,0:T(8,128)} fusion(f32[512,4,512]{2,1,0:T(4,128)S(1)} %copy-done.5, f32[512,1,512]{2,1,0:T(1,128)S(1)} %copy.65, f32[512,1,512]{2,1,0:T(1,128)S(1)} %copy.69, f32[5,512]{1,0:T(8,128)S(1)} %fusion.57, f32[512]{0:T(512)S(1)} %copy-done.25, pred[512]{0:T(512)(128)(4,1)S(1)} %copy-done.56), kind=kLoop, calls=%fused_computation.5 | loop fusion | flops 6553600 | bytes 11547136 | tf_op jit(solution)/shard_map/mul | solution.py:212
  197.3 11.1 %fusion.13 = f32[512,4,512]{2,1,0:T(4,128)S(1)} fusion(f32[512,4,512]{2,1,0:T(4,128)S(1)} %copy-done.5, f32[512,5,512]{2,1,0:T(8,128)} %fusion.3, f32[512,4,512]{2,1,0:T(4,128)S(1)} %get-tuple-element.68, f32[512,4,480]{2,1,0:T(4,128)S(1)} %bitcast.128, f32[512,4,32]{2,1,0:T(4,128)S(1)} %slice.502, f32[512,4,512]{2,1,0:T(4,128)S(1)} %get-tuple-element.67, ...), kind=kLoop, calls=%fused_computation.18 | loop fusion | flops 9437184 | bytes 33554432 | tf_op jit(solution)/shard_map/sub | solution.py:220
  215.6 32.8 %reduce-scatter.6.cloned.1.call-done = f32[13,256]{1,0:T(8,128)} async-done(((f32[13,2048]{1,0:T(8,128)}), f32[13,256]{1,0:T(8,128)}) %reduce-scatter.6.cloned.1.call-update) | async-done | bytes 13328 | tf_op jit(solution)/shard_map/reduce_scatter | solution.py:223
  251.3 10.5 %all_gather.10 = f32[18,2048]{1,0:T(8,128)S(1)} all-gather(f32[18,256]{1,0:T(8,128)S(1)} %stack.45), channel_id=1, replica_groups=mesh['vel'=8,'gx'=4] {'vel'}, dimensions={1}, use_global_device_ids=true | all-gather | bytes 165888 | tf_op jit(solution)/shard_map/all_gather | solution.py:224
  271.2 6.1 %reshape.499 = f32[512,4,512]{2,1,0:T(4,128)} reshape(f32[512,2048]{1,0:T(8,128)} %multiply_add_fusion.1) | data formatting | bytes 8388608 | tf_op jit(solution)/shard_map/reshape | solution.py:225
  277.3 6.0 %reshape_reshape.14 = f32[2,2,128,4,512]{4,3,2,1,0:T(4,128)} reshape(f32[512,2048]{1,0:T(8,128)} %multiply_add_fusion.1) | data formatting | bytes 8388608 | tf_op jit(solution)/shard_map/reshape;reshape | solution.py:197
  297.4 9.5 %fusion.29 = (f32[512,4,512]{2,1,0:T(4,128)S(1)}, f32[512,4,512]{2,1,0:T(4,128)S(1)}) fusion(f32[512,4,512]{2,1,0:T(4,128)S(1)} %copy-done.3, f32[512,4,1]{2,1,0:T(4,128)S(1)} %slice-done.2, f32[512,4,511]{2,1,0:T(4,128)S(1)} %slice.533, f32[4,512]{1,0:T(4,128)S(1)} %copy-done.18, f32[512]{0:T(512)S(1)} %copy-done.22, pred[512]{0:T(512)(128)(4,1)S(1)} %copy-done.52, ...), kind=kLoop, calls=%fused_computation.46 | loop fusion | flops 8388608 | bytes 20993024 | tf_op jit(solution)/shard_map/mul | solution.py:218
  310.7 6.9 %fusion.5 = f32[512,5,512]{2,1,0:T(8,128)} fusion(f32[512,4,512]{2,1,0:T(4,128)S(1)} %copy-done.3, f32[512,1,512]{2,1,0:T(1,128)S(1)} %copy.73, f32[512,1,512]{2,1,0:T(1,128)S(1)} %copy.77, f32[5,512]{1,0:T(8,128)S(1)} %fusion.57, f32[512]{0:T(512)S(1)} %copy-done.25, pred[512]{0:T(512)(128)(4,1)S(1)} %copy-done.56), kind=kLoop, calls=%fused_computation.8 | loop fusion | flops 6553600 | bytes 11547136 | tf_op jit(solution)/shard_map/mul | solution.py:212
  317.7 11.1 %fusion.9 = f32[512,4,512]{2,1,0:T(4,128)S(1)} fusion(f32[512,4,512]{2,1,0:T(4,128)S(1)} %copy-done.3, f32[512,5,512]{2,1,0:T(8,128)} %fusion.5, f32[512,4,512]{2,1,0:T(4,128)S(1)} %get-tuple-element.62, f32[512,4,480]{2,1,0:T(4,128)S(1)} %bitcast.126, f32[512,4,32]{2,1,0:T(4,128)S(1)} %slice.531, f32[512,4,512]{2,1,0:T(4,128)S(1)} %get-tuple-element.61, ...), kind=kLoop, calls=%fused_computation.13 | loop fusion | flops 9437184 | bytes 33554432 | tf_op jit(solution)/shard_map/sub | solution.py:220
  335.6 33.3 %reduce-scatter.8.cloned.1.call-done = f32[13,256]{1,0:T(8,128)} async-done(((f32[13,2048]{1,0:T(8,128)}), f32[13,256]{1,0:T(8,128)}) %reduce-scatter.8.cloned.1.call-update) | async-done | bytes 13328 | tf_op jit(solution)/shard_map/reduce_scatter | solution.py:223
  371.8 10.7 %all_gather.11 = f32[18,2048]{1,0:T(8,128)S(1)} all-gather(f32[18,256]{1,0:T(8,128)S(1)} %stack.50), channel_id=1, replica_groups=mesh['vel'=8,'gx'=4] {'vel'}, dimensions={1}, use_global_device_ids=true | all-gather | bytes 165888 | tf_op jit(solution)/shard_map/all_gather | solution.py:224
  386.0 5.9 %multiply_add_fusion = f32[512,2048]{1,0:T(8,128)} fusion(f32[512,2048]{1,0:T(8,128)S(1)} %bitcast.134, f32[512,2048]{1,0:T(8,128)S(1)} %fusion.51, f32[512,13]{0,1:T(8,128)S(1)} %stack.39, f32[18,2048]{1,0:T(8,128)S(1)} %all_gather.11), kind=kOutput, calls=%fused_computation.48 | convolution fusion | flops 167772160 | bytes 12746752 | tf_op jit(solution)/shard_map/dot_general | solution.py:152
  (238 shorter events, 114.8 us)
Async XLA Ops:
  6.5 120.9 %reduce-scatter.4.cloned.1.call-start = ((), (), s32[]{:S(2)}) async-start(), calls=%async_computation.3 | async-start | bytes 147456 | tf_op jit(solution)/shard_map/reduce_scatter | solution.py:223
  12.5 17.3 %copy-start.23 = (s32[16,512]{1,0:T(8,128)S(1)}, s32[16,512]{1,0:T(8,128)}, u32[]{:S(2)}) copy-start(s32[16,512]{1,0:T(8,128)} %param.5) | copy-start | bytes 98308
  19.5 46.1 %collective-permute-start = (f32[2,128,512]{2,1,0:T(8,128)}, f32[2,128,512]{2,1,0:T(8,128)}, u32[]{:S(2)}, u32[]{:S(2)}) collective-permute-start(f32[2,128,512]{2,1,0:T(8,128)} %bitcast.116), channel_id=1, source_target_pairs={{0,1},{1,2},{2,3},{4,5},{5,6},{6,7},{8,9},{9,10},{10,11},{12,13},{... | collective-permute-start | bytes 1572872 | tf_op jit(solution)/shard_map/ppermute | solution.py:21
  23.6 44.5 %collective-permute-start.1 = (f32[2,128,512]{2,1,0:T(8,128)}, f32[2,128,512]{2,1,0:T(8,128)}, u32[]{:S(2)}, u32[]{:S(2)}) collective-permute-start(f32[2,128,512]{2,1,0:T(8,128)} %bitcast.115), channel_id=1, source_target_pairs={{1,0},{2,1},{3,2},{5,4},{6,5},{7,6},{9,8},{10,9},{11,10},{13,12},{... | collective-permute-start | bytes 1572872 | tf_op jit(solution)/shard_map/ppermute | solution.py:21
  25.9 21.1 %copy-start.51 = (pred[512]{0:T(512)(128)(4,1)}, pred[512]{0:T(512)(128)(4,1)S(1)}, u32[]{:S(2)}) copy-start(pred[512]{0:T(512)(128)(4,1)S(1)} %get-tuple-element.136) | copy-start | bytes 1540
  25.9 21.1 %copy-start.53 = (pred[512]{0:T(512)(128)(4,1)}, pred[512]{0:T(512)(128)(4,1)S(1)}, u32[]{:S(2)}) copy-start(pred[512]{0:T(512)(128)(4,1)S(1)} %get-tuple-element.137) | copy-start | bytes 1540
  27.8 19.1 %copy-start.21 = (f32[512]{0:T(512)}, f32[512]{0:T(512)S(1)}, u32[]{:S(2)}) copy-start(f32[512]{0:T(512)S(1)} %get-tuple-element.129) | copy-start | bytes 6148
  47.0 12.4 %copy-start.17 = (f32[4,512]{1,0:T(4,128)}, f32[4,512]{1,0:T(4,128)S(1)}, u32[]{:S(2)}) copy-start(f32[4,512]{1,0:T(4,128)S(1)} %get-tuple-element.79) | copy-start | bytes 24580
  47.0 12.4 %copy-start.19 = (f32[4,512]{1,0:T(4,128)}, f32[4,512]{1,0:T(4,128)S(1)}, u32[]{:S(2)}) copy-start(f32[4,512]{1,0:T(4,128)S(1)} %get-tuple-element.80) | copy-start | bytes 24580
  47.0 13.1 %copy-start.57 = (s32[2,512]{1,0:T(2,128)S(1)}, s32[2,512]{1,0:T(2,128)}, u32[]{:S(2)}) copy-start(s32[2,512]{1,0:T(2,128)} %param.6) | copy-start | bytes 12292
  60.1 7.9 %copy-start.38 = (pred[512]{0:T(512)(128)(4,1)}, pred[512]{0:T(512)(128)(4,1)S(1)}, u32[]{:S(2)}) copy-start(pred[512]{0:T(512)(128)(4,1)S(1)} %get-tuple-element.6) | copy-start | bytes 1540
  60.2 7.9 %copy-start.40 = (pred[512]{0:T(512)(128)(4,1)}, pred[512]{0:T(512)(128)(4,1)S(1)}, u32[]{:S(2)}) copy-start(pred[512]{0:T(512)(128)(4,1)S(1)} %get-tuple-element.5) | copy-start | bytes 1540
  93.1 155.4 %reduce-scatter.6.cloned.1.call-start = ((), (), s32[]{:S(2)}) async-start(), calls=%async_computation.4 | async-start | bytes 147456 | tf_op jit(solution)/shard_map/reduce_scatter | solution.py:223
  130.4 14.0 %copy-start.9 = (f32[64,8,4,512]{3,1,2,0:T(8,128)S(1)}, f32[64,8,4,512]{3,1,2,0:T(8,128)}, u32[]{:S(2)}) copy-start(f32[64,8,4,512]{3,1,2,0:T(8,128)} %copy-done.8) | copy-start | bytes 12582916
  167.3 9.5 %copy-start.18 = (f32[4,512]{1,0:T(4,128)S(1)}, f32[4,512]{1,0:T(4,128)}, u32[]{:S(2)}) copy-start(f32[4,512]{1,0:T(4,128)} %copy-done.17) | copy-start | bytes 24580
  167.3 9.5 %copy-start.20 = (f32[4,512]{1,0:T(4,128)S(1)}, f32[4,512]{1,0:T(4,128)}, u32[]{:S(2)}) copy-start(f32[4,512]{1,0:T(4,128)} %copy-done.19) | copy-start | bytes 24580
  169.6 7.3 %copy-start.5 = (f32[512,4,512]{2,1,0:T(4,128)S(1)}, f32[512,4,512]{2,1,0:T(4,128)}, u32[]{:S(2)}) copy-start(f32[512,4,512]{2,1,0:T(4,128)} %reshape.495) | copy-start | bytes 12582916
  171.3 16.3 %collective-permute-start.3 = (f32[2,128,512]{2,1,0:T(8,128)S(1)}, f32[2,128,512]{2,1,0:T(8,128)S(1)}, u32[]{:S(2)}, u32[]{:S(2)}) collective-permute-start(f32[2,128,512]{2,1,0:T(8,128)S(1)} %bitcast.147), channel_id=1, source_target_pairs={{1,0},{2,1},{3,2},{5,4},{6,5},{7,6},{9,8},{10,9},{11,10},{13,12},{... | collective-permute-start | bytes 1572872 | tf_op jit(solution)/shard_map/ppermute | solution.py:21
  173.6 15.3 %collective-permute-start.2 = (f32[2,128,512]{2,1,0:T(8,128)S(1)}, f32[2,128,512]{2,1,0:T(8,128)S(1)}, u32[]{:S(2)}, u32[]{:S(2)}) collective-permute-start(f32[2,128,512]{2,1,0:T(8,128)S(1)} %bitcast.145), channel_id=1, source_target_pairs={{0,1},{1,2},{2,3},{4,5},{5,6},{6,7},{8,9},{9,10},{10,11},{12,13},{... | collective-permute-start | bytes 1572872 | tf_op jit(solution)/shard_map/ppermute | solution.py:21
  215.2 153.7 %reduce-scatter.8.cloned.1.call-start = ((), (), s32[]{:S(2)}) async-start(), calls=%async_computation.5 | async-start | bytes 147456 | tf_op jit(solution)/shard_map/reduce_scatter | solution.py:223
  251.3 14.0 %copy-start.11 = (f32[64,8,4,512]{3,1,2,0:T(8,128)S(1)}, f32[64,8,4,512]{3,1,2,0:T(8,128)}, u32[]{:S(2)}) copy-start(f32[64,8,4,512]{3,1,2,0:T(8,128)} %copy-done.10) | copy-start | bytes 12582916
  291.9 16.2 %collective-permute-start.5 = (f32[2,128,512]{2,1,0:T(8,128)S(1)}, f32[2,128,512]{2,1,0:T(8,128)S(1)}, u32[]{:S(2)}, u32[]{:S(2)}) collective-permute-start(f32[2,128,512]{2,1,0:T(8,128)S(1)} %bitcast.146), channel_id=1, source_target_pairs={{1,0},{2,1},{3,2},{5,4},{6,5},{7,6},{9,8},{10,9},{11,10},{13,12},{... | collective-permute-start | bytes 1572872 | tf_op jit(solution)/shard_map/ppermute | solution.py:21
  294.2 15.2 %collective-permute-start.4 = (f32[2,128,512]{2,1,0:T(8,128)S(1)}, f32[2,128,512]{2,1,0:T(8,128)S(1)}, u32[]{:S(2)}, u32[]{:S(2)}) collective-permute-start(f32[2,128,512]{2,1,0:T(8,128)S(1)} %bitcast.144), channel_id=1, source_target_pairs={{0,1},{1,2},{2,3},{4,5},{5,6},{6,7},{8,9},{9,10},{10,11},{12,13},{... | collective-permute-start | bytes 1572872 | tf_op jit(solution)/shard_map/ppermute | solution.py:21
  371.8 14.2 %copy-start.13 = (f32[64,8,4,512]{3,1,2,0:T(8,128)S(1)}, f32[64,8,4,512]{3,1,2,0:T(8,128)}, u32[]{:S(2)}) copy-start(f32[64,8,4,512]{3,1,2,0:T(8,128)} %copy-done.12) | copy-start | bytes 12582916
  (50 other events, 241.4 us)
Sparse Core Ops, SparseCore 0:
  93.2 34.2 reduce-scatter.3
  215.3 33.0 reduce-scatter.5
  335.7 33.1 reduce-scatter.7
where the time goes:
time: 404 us; the launch traced here: 399 us
  local copies, waits for them, and re-layouts  101 us (25%)
  waiting for transfers between devices  100 us (25%)
  other arithmetic  97.5 us (24%)
  matrix products  36.7 us (9%)
  blocking collectives  31.7 us (8%)
  starting transfers between devices  16.8 us (4%)
  between operations  14.7 us (4%)
    reduce_scatter x3, waiting for transfers between devices, per_device(): lax.psum_scatter(partial_value, 'vel', scatter_dimension=1, tiled=True)  100 us
    all_gather x3, blocking collectives, per_device(): lax.all_gather(shakhov_coefficients(owned), 'vel', axis=1, tiled=True)  31.7 us
    mul x3, other arithmetic, per_device(): speed * jnp.where(speed > 0, state, jnp.roll(state, -1, axis=2)) * open_z  31.2 us
    sub x3, other arithmetic, per_device(): moved = state - time_step * change  30.9 us
    mul x3, other arithmetic, per_device(): flux = speed * upwind * open_x  18.8 us
    another operation x3, local copies, waits for them, and re-layouts, per_device(): transport_view = state.reshape(blocks, 2, half, depth, section)  18.1 us
    dot_general x3, matrix products, relax(): jnp.dot(poly_rows, coefficients[5:18], precision=lax.Precision.HIGHEST)  18.1 us
    ppermute x6, starting transfers between devices, passed_along(): return lax.ppermute(array, axis, pairs)  16.3 us
  transfers between devices with their start and end apart: 9, of which 3 were waited for; matrix products, arithmetic and copies ran while one was open for 17% of the time, Pallas kernels for 0%

commit v1 on v0

v1 whole, which is shorter than its diff:
```python
import math

import jax
import jax.numpy as jnp
from jax import lax
from jax.experimental import pallas as pl
from jax.experimental.pallas import tpu as pltpu
from jax.sharding import PartitionSpec as P

VS = 16
NY = 16
NZ = 32
STEPS = 3
LANES = 128
FEATURES = 16
TERMS = 3
COEFS = 24

vel_limit = 4.5
time_step = 0.075
relax_rate = 0.6
viscous_thermal_ratio = 0.6666667
spacing = 2.0 * vel_limit / VS
unit = spacing / 2.0
MESH = pl.DeviceIdType.MESH
F32 = jnp.float32
BF16 = jnp.bfloat16


def features(index, cx, cy, cz):
    energy = cx * cx + cy * cy + cz * cz

    def high(value):
        return jnp.floor(value * (1.0 / 64.0)) * 64.0

    cubes = [energy * cx, energy * cy, energy * cz]
    rows = [jnp.ones_like(cx), cx, cy, cz, cx * cx, cy * cy, cz * cz, cx * cy, cx * cz, cy * cz]
    rows += [high(c) for c in cubes]
    rows += [c - high(c) for c in cubes]
    out = rows[0]
    for k in range(1, FEATURES):
        out = jnp.where(index == k, rows[k], out)
    return out


def shakhov_rows(moments):
    weight = spacing**3
    degree = [0, 1, 1, 1, 2, 2, 2, 2, 2, 2, 3, 3, 3]
    m = [moments[k : k + 1] for k in range(FEATURES)]
    m = m[:10] + [m[10 + a] + m[13 + a] for a in range(3)]
    m = [row * (weight * unit**d) for row, d in zip(m, degree)]
    n = m[0]
    inv_n = 1.0 / n
    u = [m[1] * inv_n, m[2] * inv_n, m[3] * inv_n]
    xx, yy, zz, xy, xz, yz = m[4:10]
    uu = u[0] * u[0] + u[1] * u[1] + u[2] * u[2]
    tr = xx + yy + zz
    temp = (tr * inv_n - uu) / 3.0
    press = [
        xx * u[0] + xy * u[1] + xz * u[2],
        xy * u[0] + yy * u[1] + yz * u[2],
        xz * u[0] + yz * u[1] + zz * u[2],
    ]
    q = [0.5 * (m[10 + a] - 2.0 * press[a] - u[a] * tr + 2.0 * n * uu * u[a]) for a in range(3)]
    inv_t = 1.0 / temp
    kappa = (1.0 - viscous_thermal_ratio) / (5.0 * n * temp * temp)
    s = kappa * inv_t
    uq = u[0] * q[0] + u[1] * q[1] + u[2] * q[2]
    first = jnp.log(n) - 1.5 * jnp.log(2.0 * math.pi * temp) - uu * (0.5 * inv_t)
    quad = -0.5 * inv_t
    expo = [first, u[0] * inv_t, u[1] * inv_t, u[2] * inv_t, quad, quad, quad]
    expo = [row * (math.log2(math.e) * unit**d) for row, d in zip(expo, [0, 1, 1, 1, 2, 2, 2])]
    poly = [1.0 - s * uq * uu + 5.0 * kappa * uq]
    poly += [s * (q[a] * uu + 2.0 * uq * u[a]) - 5.0 * kappa * q[a] for a in range(3)]
    poly += [-2.0 * s * q[a] * u[a] - s * uq for a in range(3)]
    poly += [-2.0 * s * (q[a] * u[b] + q[b] * u[a]) for a, b in ((0, 1), (0, 2), (1, 2))]
    poly += [s * q[a] for a in range(3)]
    poly = [row * (relax_rate * unit**d) for row, d in zip(poly, degree)]
    poly += poly[10:13]
    return jnp.concatenate(expo + [jnp.zeros_like(n)] + poly, axis=0)


def make_kernel(n_vel, n_gx, blocks, half, depth, section):
    G = STEPS
    Q = depth + G
    cells = depth * section
    piece = cells // n_vel
    tiles = section // LANES
    wide = 2 * LANES
    zh_rows = VS // 2

    def plane_of(h, q):
        return q - G if h == 1 else depth - 1 + G - q

    def kernel(
        dist, wall, kind, inflow, out,
        S, M, H, PART, GOT, CO, CG, PHI, L, RP, RS, INF,
        in_sem, out_sem, hs_sem, hr_sem, ps_sem, pr_sem, cs_sem, cr_sem, gs_sem, gr_sem,
    ):
        me = lax.axis_index("vel")
        pos = lax.axis_index("gx")
        has_left = pos > 0
        has_right = pos < n_gx - 1
        has_up = [has_right, has_left]
        has_down = [has_left, has_right]
        up = [pos + 1, pos - 1]
        down = [pos - 1, pos + 1]

        def columns(x):
            return pl.ds(x * section, section)

        loads = {}
        for q in range(Q - 1, G - 1, -1):
            for h in range(2):
                copy = pltpu.make_async_copy(
                    dist.at[:, h, :, columns(plane_of(h, q))], S.at[h, q], in_sem.at[h, q - G]
                )
                copy.start()
                loads[h, q] = copy

        barrier = pltpu.get_barrier_semaphore()
        for d in range(1, n_vel):
            pl.semaphore_signal(
                barrier, inc=1, device_id={"vel": lax.rem(me + d, n_vel)}, device_id_type=MESH
            )
        for h in range(2):
            @pl.when(has_down[h])
            def _(h=h):
                pl.semaphore_signal(barrier, inc=1, device_id={"gx": down[h]}, device_id_type=MESH)
        met = n_vel - 1 + has_left.astype(jnp.int32) + has_right.astype(jnp.int32)
        pl.semaphore_wait(barrier, met)

        def halo(h, k):
            x = depth - 1 - k if h == 1 else k
            return pltpu.make_async_remote_copy(
                src_ref=dist.at[:, h, :, columns(x)],
                dst_ref=S.at[h, G - 1 - k],
                send_sem=hs_sem.at[h, k],
                recv_sem=hr_sem.at[h, k],
                device_id={"gx": down[h]},
                device_id_type=MESH,
            )

        def start_halo(k):
            for h in range(2):
                @pl.when(has_down[h])
                def _(h=h):
                    halo(h, k).start()

        def finish_halo_send(k):
            for h in range(2):
                @pl.when(has_down[h])
                def _(h=h):
                    halo(h, k).wait_send()

        start_halo(0)

        first_iy = me * blocks
        lane = lax.broadcasted_iota(jnp.int32, (1, section), 1)
        y_at = lane // NZ
        z_at = lane % NZ
        vy_up = first_iy >= VS // 2
        n_planes = wall.shape[0]

        def openness(x):
            at = pos * depth + x
            row = wall[pl.ds(jnp.clip(at, 0, n_planes - 1), 1), :]
            inside = jnp.logical_and(at >= 0, at < n_planes)
            return jnp.where(inside, (1 - row).astype(F32), 1.0)

        for h in range(2):
            way = 1 if h == 1 else -1
            for q in range(1, Q):
                x = plane_of(h, q)
                o = openness(x)
                x_in = o * openness(x - way)
                x_out = o * openness(x + way)
                y_hi = jnp.where(y_at < NY - 1, o * pltpu.roll(o, section - NZ, 1), 0.0)
                y_lo = jnp.where(y_at > 0, o * pltpu.roll(o, NZ, 1), 0.0)
                z_hi = jnp.where(z_at < NZ - 1, o * pltpu.roll(o, section - 1, 1), 0.0)
                z_lo = jnp.where(z_at > 0, o * pltpu.roll(o, 1, 1), 0.0)
                y_in = jnp.where(vy_up, y_lo, y_hi)
                y_out = jnp.where(vy_up, y_hi, y_lo)
                rows = [x_in, x_out, y_in, y_out, z_hi, z_lo, z_lo, z_hi]
                H[h, q] = jnp.concatenate([r * time_step for r in rows], axis=0)

        for h in range(2):
            sign = 1.0 if h == 1 else -1.0
            shape = (FEATURES, blocks * half)
            r = lax.broadcasted_iota(jnp.int32, shape, 1)
            index = lax.broadcasted_iota(jnp.int32, shape, 0)
            cx = sign * (2 * ((r % half) // VS) + 1).astype(F32)
            cz = (2 * (r % VS) - (VS - 1)).astype(F32)
            cy = (2 * (first_iy + r // half) - (VS - 1)).astype(F32)
            PHI[h] = features(index, cx, cy, cz).astype(BF16)
            shape = (half, FEATURES * TERMS)
            r = lax.broadcasted_iota(jnp.int32, shape, 0)
            index = lax.broadcasted_iota(jnp.int32, shape, 1) % FEATURES
            cx = sign * (2 * (r // VS) + 1).astype(F32)
            cz = (2 * (r % VS) - (VS - 1)).astype(F32)
            for b in range(blocks):
                cy = jnp.full(shape, 2 * (first_iy + b) - (VS - 1), jnp.int32).astype(F32)
                L[h, b] = features(index, cx, cy, cz).astype(BF16)
                row = inflow[2 * b + h : 2 * b + h + 1, :]
                INF[h, b] = jnp.broadcast_to(row, (half, half)).T

        lane_t = lax.broadcasted_iota(jnp.int32, (zh_rows, LANES), 1)
        sub = lax.broadcasted_iota(jnp.int32, (zh_rows, LANES), 0).astype(F32)
        y_take = jnp.where(vy_up, LANES - NZ, 0)
        from_next = jnp.logical_and(lane_t >= y_take, lane_t < y_take + NZ)
        y_shift = jnp.where(vy_up, NZ, LANES - NZ)
        t_step = jnp.where(vy_up, tiles - 1, 1)

        def transport(h_list, q0, nq):
            per_h = nq * blocks * tiles

            def body(j, carry):
                if len(h_list) == 2:
                    h = j // per_h
                else:
                    h = h_list[0]
                rest = j % per_h
                q = q0 + rest // (blocks * tiles)
                b = (rest // tiles) % blocks
                t = rest % tiles
                at = pl.ds(pl.multiple_of(t * LANES, LANES), LANES)
                t_next = (t + t_step) % tiles
                at_next = pl.ds(pl.multiple_of(t_next * LANES, LANES), LANES)
                speed_y = jnp.abs(-vel_limit + ((first_iy + b).astype(F32) + 0.5) * spacing)

                def face(k):
                    return jnp.broadcast_to(H[h, q, k : k + 1, at], (zh_rows, LANES))

                x_in, x_out = face(0), face(1)
                y_in = face(2) * speed_y
                y_keep = 1.0 - face(3) * speed_y
                for zh in range(2):
                    if zh == 0:
                        speed_z = vel_limit - (sub + 0.5) * spacing
                    else:
                        speed_z = (sub + 0.5) * spacing
                    z_in = face(4 + 2 * zh) * speed_z
                    keep = y_keep - face(5 + 2 * zh) * speed_z
                    for i in range(half // VS):
                        rows = pl.ds(i * VS + zh * zh_rows, zh_rows)
                        speed_x = (i + 0.5) * spacing
                        f = S[h, q, b, rows, at]
                        before = S[h, q - 1, b, rows, at]
                        beside = S[h, q, b, rows, at_next]
                        f_y = pltpu.roll(jnp.where(from_next, beside, f), y_shift, 1)
                        f_z = pltpu.roll(f, 1 if zh == 1 else LANES - 1, 1)
                        moved = f * (keep - x_out * speed_x) + before * (x_in * speed_x)
                        moved = moved + (f_y * y_in + f_z * z_in)
                        M[h, q, b, rows, at] = moved
                return carry

            lax.fori_loop(0, len(h_list) * per_h, body, 0)

        def moments(h, q):
            halves = []
            for c in range(section // wide):
                value = M[h, q, :, :, c * wide : (c + 1) * wide].reshape(blocks * half, wide)
                hi = value.astype(BF16)
                lo = (value - hi.astype(F32)).astype(BF16)
                phi = PHI[h]
                halves.append(
                    jnp.dot(phi, hi, preferred_element_type=F32)
                    + jnp.dot(phi, lo, preferred_element_type=F32)
                )
            return halves

        def load_coefficients(rows):
            terms = []
            rest = rows
            for j in range(TERMS):
                term = rest.astype(BF16)
                terms.append(term)
                rest = rest - term.astype(F32)
            for j in range(TERMS):
                at = slice(j * FEATURES, (j + 1) * FEATURES)
                RP[at, :] = jnp.concatenate(
                    [terms[j][0:8], jnp.zeros((8, section), BF16)], axis=0
                )
                RS[at, :] = terms[j][8:COEFS]

        def relax(h, q):
            def body(j, carry):
                b = j // (section // wide)
                c = j % (section // wide)
                at = pl.ds(pl.multiple_of(c * wide, wide), wide)
                left = L[h, b]
                power = jnp.dot(left, RP[:, at], preferred_element_type=F32)
                shape = jnp.dot(left, RS[:, at], preferred_element_type=F32)
                S[h, q, b, :, at] = (1.0 - relax_rate) * M[h, q, b, :, at] + jnp.exp2(power) * shape
                return carry

            lax.fori_loop(0, blocks * (section // wide), body, 0)

        def fill_edge(h):
            inner = kind[1 - h : 2 - h, :] == 1

            for b in range(blocks):
                for t in range(tiles):
                    at = slice(t * LANES, (t + 1) * LANES)
                    S[h, G - 1, b, :, at] = jnp.where(
                        inner[:, at], INF[h, b], S[h, G, b, :, at]
                    )

        def advance_ghost(h, q, step):
            transport([h], q, 1)
            load_coefficients(CG[step, h, :, (G - 1 - q) * section : (G - q) * section])
            relax(h, q)

        def ghost_coefficients(step, h):
            planes = STEPS - 1 - step
            if h == 1:
                parts = [depth - 1 - k for k in range(planes)]
            else:
                parts = list(range(planes))
            return [
                pltpu.make_async_remote_copy(
                    src_ref=CO.at[step, :, columns(x)],
                    dst_ref=CG.at[step, h, :, columns(k)],
                    send_sem=gs_sem.at[step, h, k],
                    recv_sem=gr_sem.at[step, h, k],
                    device_id={"gx": down[h]},
                    device_id_type=MESH,
                )
                for k, x in enumerate(parts)
            ]

        own = pl.ds(pl.multiple_of(me * piece, piece), piece)
        stores = []
        for step in range(STEPS):
            last = step + 1 == STEPS
            if step == 0:
                for copy in loads.values():
                    copy.wait()
            transport([0, 1], G + 1, depth - 1)
            for x in range(depth):
                total = None
                for h in range(2):
                    q = x + G if h == 1 else depth - 1 + G - x
                    if q > G:
                        term = moments(h, q)
                        total = term if total is None else [a + b for a, b in zip(total, term)]
                for c, value in enumerate(total):
                    start = x * section + c * wide
                    PART[step, :, start : start + wide] = value

            for h in range(2):
                @pl.when(has_up[h])
                def _(h=h):
                    halo(h, step).wait_recv()
            finish_halo_send(step)
            if not last:
                start_halo(step + 1)
            for h in range(2):
                @pl.when(has_up[h])
                def _(h=h):
                    if step > 0:
                        if step == 1:
                            for copy in ghost_coefficients(0, h):
                                copy.wait_recv()
                        elif step - 1 < STEPS - 1:
                            for copy in ghost_coefficients(step - 1, h):
                                copy.wait_recv()
                        for level in range(step):
                            advance_ghost(h, G - step + level, level)

                @pl.when(jnp.logical_not(has_up[h]))
                def _(h=h):
                    fill_edge(h)

            transport([0, 1], G, 1)
            for h in range(2):
                x = plane_of(h, G)
                for c, value in enumerate(moments(h, G)):
                    at = slice(x * section + c * wide, x * section + (c + 1) * wide)
                    PART[step, :, at] = PART[step, :, at] + value

            sends = []
            for d in range(1, n_vel):
                to = lax.rem(me + d, n_vel)
                copy = pltpu.make_async_remote_copy(
                    src_ref=PART.at[step, :, pl.ds(pl.multiple_of(to * piece, piece), piece)],
                    dst_ref=GOT.at[step, d],
                    send_sem=ps_sem.at[step, d],
                    recv_sem=pr_sem.at[step, d],
                    device_id={"vel": to},
                    device_id_type=MESH,
                )
                copy.start()
                sends.append(copy)
            total = PART[step, :, own]
            for d in range(1, n_vel):
                sends[d - 1].wait_recv()
                total = total + GOT[step, d]
            CO[step, :, own] = shakhov_rows(total)
            gathers = []
            for d in range(1, n_vel):
                to = lax.rem(me + d, n_vel)
                copy = pltpu.make_async_remote_copy(
                    src_ref=CO.at[step, :, own],
                    dst_ref=CO.at[step, :, own],
                    send_sem=cs_sem.at[step, d],
                    recv_sem=cr_sem.at[step, d],
                    device_id={"vel": to},
                    device_id_type=MESH,
                )
                copy.start()
                gathers.append(copy)
            for copy in gathers:
                copy.wait_recv()
            if not last:
                for h in range(2):
                    @pl.when(has_down[h])
                    def _(h=h):
                        for copy in ghost_coefficients(step, h):
                            copy.start()
            for x in range(depth):
                load_coefficients(CO[step, :, x * section : (x + 1) * section])
                for h in range(2):
                    q = x + G if h == 1 else depth - 1 + G - x
                    relax(h, q)
                    if last:
                        copy = pltpu.make_async_copy(
                            S.at[h, q], out.at[:, h, :, columns(x)], out_sem.at[h, x]
                        )
                        copy.start()
                        stores.append(copy)
            for copy in sends + gathers:
                copy.wait_send()
            if not last:
                for h in range(2):
                    @pl.when(has_down[h])
                    def _(h=h):
                        for copy in ghost_coefficients(step, h):
                            copy.wait_send()
        for copy in stores:
            copy.wait()

    dma = pltpu.SemaphoreType.DMA
    scratch = [
        pltpu.VMEM((2, Q, blocks, half, section), F32),
        pltpu.VMEM((2, Q, blocks, half, section), F32),
        pltpu.VMEM((2, Q, 8, section), F32),
        pltpu.VMEM((STEPS, FEATURES, cells), F32),
        pltpu.VMEM((STEPS, n_vel, FEATURES, piece), F32),
        pltpu.VMEM((STEPS, COEFS, cells), F32),
        pltpu.VMEM((STEPS, 2, COEFS, (STEPS - 1) * section), F32),
        pltpu.VMEM((2, FEATURES, blocks * half), BF16),
        pltpu.VMEM((2, blocks, half, FEATURES * TERMS), BF16),
        pltpu.VMEM((FEATURES * TERMS, section), BF16),
        pltpu.VMEM((FEATURES * TERMS, section), BF16),
        pltpu.VMEM((2, blocks, half, half), F32),
        dma((2, depth)),
        dma((2, depth)),
        dma((2, STEPS)),
        dma((2, STEPS)),
        dma((STEPS, n_vel)),
        dma((STEPS, n_vel)),
        dma((STEPS, n_vel)),
        dma((STEPS, n_vel)),
        dma((STEPS, 2, STEPS)),
        dma((STEPS, 2, STEPS)),
    ]
    return kernel, scratch


def solution(mesh):
    n_vel = mesh.shape["vel"]
    n_gx = mesh.shape["gx"]

    def per_device(distribution, wall_mask, boundary_kind, inflow):
        rows, cells = distribution.shape
        section = wall_mask.shape[1]
        half = VS * VS // 2
        blocks = rows // (2 * half)
        depth = cells // section
        kernel, scratch = make_kernel(n_vel, n_gx, blocks, half, depth, section)
        vmem = pl.BlockSpec(memory_space=pltpu.VMEM)
        out = pl.pallas_call(
            kernel,
            out_shape=jax.ShapeDtypeStruct((blocks, 2, half, cells), F32),
            in_specs=[pl.BlockSpec(memory_space=pl.ANY), vmem, vmem, vmem],
            out_specs=pl.BlockSpec(memory_space=pl.ANY),
            scratch_shapes=scratch,
            compiler_params=pltpu.CompilerParams(
                collective_id=0, has_side_effects=True, vmem_limit_bytes=48 * 1024 * 1024
            ),
        )(
            distribution.reshape(blocks, 2, half, cells),
            wall_mask,
            boundary_kind,
            inflow.reshape(2 * blocks, half),
        )
        return out.reshape(rows, cells)

    placed = (P("vel", "gx"), P(), P(), P("vel"))
    return jax.shard_map(
        per_device, mesh=mesh, in_specs=placed, out_specs=P("vel", "gx"), check_vma=False
    )
```

time: 404 us -> 94.3 us (0.23); the launches traced: 399 us -> 93.8 us
  waiting for transfers between devices: 100 us -> 0 us
  other arithmetic: 97.5 us -> 0 us
  local copies, waits for them, and re-layouts: 101 us -> 4.14 us
  Pallas kernels: 0 us -> 89.7 us
  matrix products: 36.7 us -> 0 us
  blocking collectives: 31.7 us -> 0 us
  starting transfers between devices: 16.8 us -> 0 us
  between operations: 14.7 us -> 0.01 us
    reduce_scatter x3 -> x0, waiting for transfers between devices: 100 us -> none  [per_device(): lax.psum_scatter(partial_value, 'vel', scatter_dimension=1, tiled=True)]
    pallas_call x0 -> x1, Pallas kernels: none -> 89.7 us  [per_device(): pl.pallas_call(kernel, out_shape=jax.ShapeDtypeStruct((blocks, 2, half, c...]
    mul x18 -> x0, other arithmetic: 58.5 us -> none  [the longest x3 31.2 us: per_device(): speed * jnp.where(speed > 0, state, jnp.roll(state, -1, axis=2)) * open_z]
    slice x32 -> x0, local copies, waits for them, and re-layouts: 41 us -> none  [the longest x9 15.8 us: per_device(): jnp.roll(state, -1, axis=2)]
    dot_general x9 -> x0, matrix products: 36.7 us -> none  [the longest x3 18.1 us: relax(): jnp.dot(poly_rows, coefficients[5:18], precision=lax.Precision.HIGHEST)]
    sub x12 -> x0, other arithmetic: 33.6 us -> none  [the longest x3 30.9 us: per_device(): moved = state - time_step * change]
    all_gather x3 -> x0, blocking collectives: 31.7 us -> none  [per_device(): lax.all_gather(shakhov_coefficients(owned), 'vel', axis=1, tiled=True)]
    reshape x9 -> x0, local copies, waits for them, and re-layouts: 24.6 us -> none  [the longest x2 12.1 us: per_device(): relax(moved2, coefficients, expo, poly).reshape(rows_dev, depth, section)]
  transfers between devices with their start and end apart: 9 -> 0, of which waited for: 3 -> 0; matrix products, arithmetic and copies ran while one was open for 17% -> 0% of each run, Pallas kernels for 0% -> 0%
where the time goes in v1:
time: 94.3 us; the launch traced here: 93.8 us
  Pallas kernels  89.7 us (95%)
  local copies, waits for them, and re-layouts  4.14 us (4%)
    pallas_call x1, Pallas kernels, per_device(): pl.pallas_call(kernel, out_shape=jax.ShapeDtypeStruct((blocks, 2, half, c...  89.7 us
    unnamed x7, local copies, waits for them, and re-layouts  4.14 us

profile of v1, /device:TPU:17, one launch (start us, length us, event | category | flops | bytes accessed | tf_op | source)
XLA Modules:
  0.0 93.8 jit_solution(2054928695353392148)
XLA Ops:
  0.0 0.0 copy-start
  0.0 0.8 copy-done
  0.8 0.0 copy-start.1
  0.8 0.7 copy-done.1
  1.4 0.0 copy-start.2
  1.4 0.7 copy-done.2
  2.1 89.7 %shard_map.46 = f32[2,2,128,2048]{3,2,1,0:T(8,128)S(1)} custom-call(f32[2,2,128,2048]{3,2,1,0:T(8,128)} %bitcast.5, s32[16,512]{1,0:T(8,128)S(1)} %copy-done, s32[2,512]{1,0:T(2,128)S(1)} %copy-done.1, f32[4,128]{1,0:T(4,128)S(1)} %bitcast.4), custom_call_target="tpu_custom_call" | custom-call | tf_op jit(solution)/shard_map/pallas_call | solution.py:483
  91.8 2.0 %copy.6 = f32[512,2048]{1,0:T(8,128)} copy(f32[512,2048]{1,0:T(8,128)S(1)} %bitcast.3) | data formatting | bytes 8388608
Async XLA Ops:
  0.0 0.8 copy-start
  0.8 0.7 copy-start.1
  1.4 0.7 copy-start.2

commit v2 on v1

--- a/solution.py
+++ b/solution.py
@@ -80,7 +80,7 @@
     return jnp.concatenate(expo + [jnp.zeros_like(n)] + poly, axis=0)
 
 
-def make_kernel(n_vel, n_gx, blocks, half, depth, section):
+def make_kernel(n_vel, n_gx, blocks, half, depth, section, planes):
     G = STEPS
     Q = depth + G
     cells = depth * section
@@ -93,8 +93,8 @@
         return q - G if h == 1 else depth - 1 + G - q
 
     def kernel(
-        dist, wall, kind, inflow, out,
-        S, M, H, PART, GOT, CO, CG, PHI, L, RP, RS, INF,
+        dist, wall_in, kind_in, inflow_in, out,
+        S, M, H, PART, GOT, CO, CG, PHI, L, RP, RS, INF, wall, kind, inflow, sm_sem,
         in_sem, out_sem, hs_sem, hr_sem, ps_sem, pr_sem, cs_sem, cr_sem, gs_sem, gr_sem,
     ):
         me = lax.axis_index("vel")
@@ -117,6 +117,12 @@
                 )
                 copy.start()
                 loads[h, q] = copy
+
+        small = []
+        for k, (src, dst) in enumerate(((wall_in, wall), (kind_in, kind), (inflow_in, inflow))):
+            copy = pltpu.make_async_copy(src, dst, sm_sem.at[k])
+            copy.start()
+            small.append(copy)
 
         barrier = pltpu.get_barrier_semaphore()
         for d in range(1, n_vel):
@@ -154,6 +160,9 @@
                     halo(h, k).wait_send()
 
         start_halo(0)
+
+        for copy in small:
+            copy.wait()
 
         first_iy = me * blocks
         lane = lax.broadcasted_iota(jnp.int32, (1, section), 1)
@@ -212,49 +221,46 @@
         t_step = jnp.where(vy_up, tiles - 1, 1)
 
         def transport(h_list, q0, nq):
-            per_h = nq * blocks * tiles
+            nh = len(h_list)
 
             def body(j, carry):
-                if len(h_list) == 2:
-                    h = j // per_h
-                else:
-                    h = h_list[0]
-                rest = j % per_h
-                q = q0 + rest // (blocks * tiles)
-                b = (rest // tiles) % blocks
-                t = rest % tiles
-                at = pl.ds(pl.multiple_of(t * LANES, LANES), LANES)
-                t_next = (t + t_step) % tiles
-                at_next = pl.ds(pl.multiple_of(t_next * LANES, LANES), LANES)
+                b = lax.rem(j, blocks)
+                outer = lax.div(j, blocks)
+                h = lax.rem(outer, nh) if nh == 2 else h_list[0]
+                q = q0 + lax.div(outer, nh)
                 speed_y = jnp.abs(-vel_limit + ((first_iy + b).astype(F32) + 0.5) * spacing)
-
-                def face(k):
-                    return jnp.broadcast_to(H[h, q, k : k + 1, at], (zh_rows, LANES))
-
-                x_in, x_out = face(0), face(1)
-                y_in = face(2) * speed_y
-                y_keep = 1.0 - face(3) * speed_y
-                for zh in range(2):
-                    if zh == 0:
-                        speed_z = vel_limit - (sub + 0.5) * spacing
-                    else:
-                        speed_z = (sub + 0.5) * spacing
-                    z_in = face(4 + 2 * zh) * speed_z
-                    keep = y_keep - face(5 + 2 * zh) * speed_z
-                    for i in range(half // VS):
-                        rows = pl.ds(i * VS + zh * zh_rows, zh_rows)
-                        speed_x = (i + 0.5) * spacing
-                        f = S[h, q, b, rows, at]
-                        before = S[h, q - 1, b, rows, at]
-                        beside = S[h, q, b, rows, at_next]
-                        f_y = pltpu.roll(jnp.where(from_next, beside, f), y_shift, 1)
-                        f_z = pltpu.roll(f, 1 if zh == 1 else LANES - 1, 1)
-                        moved = f * (keep - x_out * speed_x) + before * (x_in * speed_x)
-                        moved = moved + (f_y * y_in + f_z * z_in)
-                        M[h, q, b, rows, at] = moved
+                for t in range(tiles):
+                    at = slice(t * LANES, (t + 1) * LANES)
+                    t_next = lax.rem(t + t_step, tiles)
+                    at_next = pl.ds(pl.multiple_of(t_next * LANES, LANES), LANES)
+
+                    def face(k):
+                        return jnp.broadcast_to(H[h, q, k : k + 1, at], (zh_rows, LANES))
+
+                    x_in, x_out = face(0), face(1)
+                    y_in = face(2) * speed_y
+                    y_keep = 1.0 - face(3) * speed_y
+                    for zh in range(2):
+                        if zh == 0:
+                            speed_z = vel_limit - (sub + 0.5) * spacing
+                        else:
+                            speed_z = (sub + 0.5) * spacing
+                        z_in = face(4 + 2 * zh) * speed_z
+                        keep = y_keep - face(5 + 2 * zh) * speed_z
+                        for i in range(half // VS):
+                            rows = pl.ds(i * VS + zh * zh_rows, zh_rows)
+                            speed_x = (i + 0.5) * spacing
+                            f = S[h, q, b, rows, at]
+                            before = S[h, q - 1, b, rows, at]
+                            beside = S[h, q, b, rows, at_next]
+                            f_y = pltpu.roll(jnp.where(from_next, beside, f), y_shift, 1)
+                            f_z = pltpu.roll(f, 1 if zh == 1 else LANES - 1, 1)
+                            moved = f * (keep - x_out * speed_x) + before * (x_in * speed_x)
+                            moved = moved + (f_y * y_in + f_z * z_in)
+                            M[h, q, b, rows, at] = moved
                 return carry
 
-            lax.fori_loop(0, len(h_list) * per_h, body, 0)
+            lax.fori_loop(0, nh * nq * blocks, body, 0)
 
         def moments(h, q):
             halves = []
@@ -269,7 +275,7 @@
                 )
             return halves
 
-        def load_coefficients(rows):
+        def load_coefficients(rows, slot):
             terms = []
             rest = rows
             for j in range(TERMS):
@@ -278,23 +284,19 @@
                 rest = rest - term.astype(F32)
             for j in range(TERMS):
                 at = slice(j * FEATURES, (j + 1) * FEATURES)
-                RP[at, :] = jnp.concatenate(
+                RP[slot, at, :] = jnp.concatenate(
                     [terms[j][0:8], jnp.zeros((8, section), BF16)], axis=0
                 )
-                RS[at, :] = terms[j][8:COEFS]
-
-        def relax(h, q):
-            def body(j, carry):
-                b = j // (section // wide)
-                c = j % (section // wide)
-                at = pl.ds(pl.multiple_of(c * wide, wide), wide)
-                left = L[h, b]
-                power = jnp.dot(left, RP[:, at], preferred_element_type=F32)
-                shape = jnp.dot(left, RS[:, at], preferred_element_type=F32)
-                S[h, q, b, :, at] = (1.0 - relax_rate) * M[h, q, b, :, at] + jnp.exp2(power) * shape
-                return carry
-
-            lax.fori_loop(0, blocks * (section // wide), body, 0)
+                RS[slot, at, :] = terms[j][8:COEFS]
+
+        def relax(h, q, slot):
+            for c in range(section // wide):
+                at = slice(c * wide, (c + 1) * wide)
+                left = L[h].reshape(blocks * half, FEATURES * TERMS)
+                power = jnp.dot(left, RP[slot, :, at], preferred_element_type=F32)
+                shape = jnp.dot(left, RS[slot, :, at], preferred_element_type=F32)
+                fresh = (jnp.exp2(power) * shape).reshape(blocks, half, wide)
+                S[h, q, :, :, at] = (1.0 - relax_rate) * M[h, q, :, :, at] + fresh
 
         def fill_edge(h):
             inner = kind[1 - h : 2 - h, :] == 1
@@ -308,15 +310,15 @@
 
         def advance_ghost(h, q, step):
             transport([h], q, 1)
-            load_coefficients(CG[step, h, :, (G - 1 - q) * section : (G - q) * section])
-            relax(h, q)
+            load_coefficients(CG[step, h, :, (G - 1 - q) * section : (G - q) * section], 0)
+            relax(h, q, 0)
 
         def ghost_coefficients(step, h):
-            planes = STEPS - 1 - step
+            ghosts = STEPS - 1 - step
             if h == 1:
-                parts = [depth - 1 - k for k in range(planes)]
+                parts = [depth - 1 - k for k in range(ghosts)]
             else:
-                parts = list(range(planes))
+                parts = list(range(ghosts))
             return [
                 pltpu.make_async_remote_copy(
                     src_ref=CO.at[step, :, columns(x)],
@@ -419,10 +421,10 @@
                         for copy in ghost_coefficients(step, h):
                             copy.start()
             for x in range(depth):
-                load_coefficients(CO[step, :, x * section : (x + 1) * section])
+                load_coefficients(CO[step, :, x * section : (x + 1) * section], x % 2)
                 for h in range(2):
                     q = x + G if h == 1 else depth - 1 + G - x
-                    relax(h, q)
+                    relax(h, q, x % 2)
                     if last:
                         copy = pltpu.make_async_copy(
                             S.at[h, q], out.at[:, h, :, columns(x)], out_sem.at[h, x]
@@ -451,9 +453,13 @@
         pltpu.VMEM((STEPS, 2, COEFS, (STEPS - 1) * section), F32),
         pltpu.VMEM((2, FEATURES, blocks * half), BF16),
         pltpu.VMEM((2, blocks, half, FEATURES * TERMS), BF16),
-        pltpu.VMEM((FEATURES * TERMS, section), BF16),
-        pltpu.VMEM((FEATURES * TERMS, section), BF16),
+        pltpu.VMEM((2, FEATURES * TERMS, section), BF16),
+        pltpu.VMEM((2, FEATURES * TERMS, section), BF16),
         pltpu.VMEM((2, blocks, half, half), F32),
+        pltpu.VMEM((planes, section), jnp.int32),
+        pltpu.VMEM((2, section), jnp.int32),
+        pltpu.VMEM((2 * blocks, half), F32),
+        dma((3,)),
         dma((2, depth)),
         dma((2, depth)),
         dma((2, STEPS)),
@@ -478,13 +484,13 @@
         half = VS * VS // 2
         blocks = rows // (2 * half)
         depth = cells // section
-        kernel, scratch = make_kernel(n_vel, n_gx, blocks, half, depth, section)
-        vmem = pl.BlockSpec(memory_space=pltpu.VMEM)
+        kernel, scratch = make_kernel(n_vel, n_gx, blocks, half, depth, section, wall_mask.shape[0])
+        whole = pl.BlockSpec(memory_space=pl.ANY)
         out = pl.pallas_call(
             kernel,
             out_shape=jax.ShapeDtypeStruct((blocks, 2, half, cells), F32),
-            in_specs=[pl.BlockSpec(memory_space=pl.ANY), vmem, vmem, vmem],
-            out_specs=pl.BlockSpec(memory_space=pl.ANY),
+            in_specs=[whole] * 4,
+            out_specs=whole,
             scratch_shapes=scratch,
             compiler_params=pltpu.CompilerParams(
                 collective_id=0, has_side_effects=True, vmem_limit_bytes=48 * 1024 * 1024

time: 94.3 us -> 68.3 us (0.72)
  Pallas kernels: 89.7 us -> 63.9 us
    pallas_call x1, Pallas kernels: 89.7 us -> 63.9 us  [per_device(): pl.pallas_call(kernel, out_shape=jax.ShapeDtypeStruct((blocks, 2, half, c...]
where the time goes in v2:
time: 68.3 us; the launch traced here: 68.1 us
  Pallas kernels  63.9 us (94%)
  local copies, waits for them, and re-layouts  4.14 us (6%)
    pallas_call x1, Pallas kernels, per_device(): pl.pallas_call(kernel, out_shape=jax.ShapeDtypeStruct((blocks, 2, half, c...  63.9 us
    unnamed x7, local copies, waits for them, and re-layouts  4.14 us

profile of v2, /device:TPU:17, one launch (start us, length us, event | category | flops | bytes accessed | tf_op | source)
XLA Modules:
  0.0 68.1 jit_solution(10929407268365954770)
XLA Ops:
  0.0 0.0 copy-start
  0.0 0.8 %copy-done = s32[16,512]{1,0:T(8,128)S(1)} copy-done((s32[16,512]{1,0:T(8,128)S(1)}, s32[16,512]{1,0:T(8,128)}, u32[]{:S(2)}) %copy-start) | copy-done | bytes 32792
  0.8 0.0 copy-start.1
  0.8 0.7 %copy-done.1 = s32[2,512]{1,0:T(2,128)S(1)} copy-done((s32[2,512]{1,0:T(2,128)S(1)}, s32[2,512]{1,0:T(2,128)}, u32[]{:S(2)}) %copy-start.1) | copy-done | bytes 4120
  1.4 0.0 copy-start.2
  1.4 0.7 copy-done.2
  2.1 63.9 %shard_map.46 = f32[2,2,128,2048]{3,2,1,0:T(8,128)S(1)} custom-call(f32[2,2,128,2048]{3,2,1,0:T(8,128)} %bitcast.5, s32[16,512]{1,0:T(8,128)S(1)} %copy-done, s32[2,512]{1,0:T(2,128)S(1)} %copy-done.1, f32[4,128]{1,0:T(4,128)S(1)} %bitcast.4), custom_call_target="tpu_custom_call" | custom-call | tf_op jit(solution)/shard_map/pallas_call | solution.py:489
  66.0 2.0 %copy.6 = f32[512,2048]{1,0:T(8,128)} copy(f32[512,2048]{1,0:T(8,128)S(1)} %bitcast.3) | data formatting | bytes 8388608
Async XLA Ops:
  0.0 0.8 %copy-start = (s32[16,512]{1,0:T(8,128)S(1)}, s32[16,512]{1,0:T(8,128)}, u32[]{:S(2)}) copy-start(s32[16,512]{1,0:T(8,128)} %wall_in.1) | copy-start | bytes 98308
  0.8 0.7 %copy-start.1 = (s32[2,512]{1,0:T(2,128)S(1)}, s32[2,512]{1,0:T(2,128)}, u32[]{:S(2)}) copy-start(s32[2,512]{1,0:T(2,128)} %kind_in.1) | copy-start | bytes 12292
  1.4 0.7 %copy-start.2 = (f32[512]{0:T(512)S(1)}, f32[512]{0:T(512)}, u32[]{:S(2)}) copy-start(f32[512]{0:T(512)} %param.7) | copy-start | bytes 6148

commit v3 on v2

--- a/solution.py
+++ b/solution.py
@@ -84,7 +84,12 @@
     G = STEPS
     Q = depth + G
     cells = depth * section
-    piece = cells // n_vel
+    groups = [list(range(1, depth - 1)), [0, depth - 1]]
+    if len(groups[0]) != len(groups[1]) or cells // 2 % (n_vel * LANES):
+        groups = [list(range(depth))]
+    order = [x for group in groups for x in group]
+    span = cells // len(groups)
+    piece = span // n_vel
     tiles = section // LANES
     wide = 2 * LANES
     zh_rows = VS // 2
@@ -108,6 +113,12 @@
 
         def columns(x):
             return pl.ds(x * section, section)
+
+        def place(x):
+            return pl.ds(order.index(x) * section, section)
+
+        def q_of(h, x):
+            return x + G if h == 1 else depth - 1 + G - x
 
         loads = {}
         for q in range(Q - 1, G - 1, -1):
@@ -321,7 +332,7 @@
                 parts = list(range(ghosts))
             return [
                 pltpu.make_async_remote_copy(
-                    src_ref=CO.at[step, :, columns(x)],
+                    src_ref=CO.at[step, :, place(x)],
                     dst_ref=CG.at[step, h, :, columns(k)],
                     send_sem=gs_sem.at[step, h, k],
                     recv_sem=gr_sem.at[step, h, k],
@@ -331,24 +342,117 @@
                 for k, x in enumerate(parts)
             ]
 
-        own = pl.ds(pl.multiple_of(me * piece, piece), piece)
+        def share(g, who):
+            return pl.ds(pl.multiple_of(g * span + who * piece, piece), piece)
+
+        def store_moments(step, x, values):
+            for c, value in enumerate(values):
+                start = order.index(x) * section + c * wide
+                PART[step, :, start : start + wide] = value
+
+        def add_moments(step, x, values):
+            for c, value in enumerate(values):
+                start = order.index(x) * section + c * wide
+                at = slice(start, start + wide)
+                PART[step, :, at] = PART[step, :, at] + value
+
+        def send_moments(step, g):
+            copies = []
+            for d in range(1, n_vel):
+                to = lax.rem(me + d, n_vel)
+                copy = pltpu.make_async_remote_copy(
+                    src_ref=PART.at[step, :, share(g, to)],
+                    dst_ref=GOT.at[step, g, d],
+                    send_sem=ps_sem.at[step, g, d],
+                    recv_sem=pr_sem.at[step, g, d],
+                    device_id={"vel": to},
+                    device_id_type=MESH,
+                )
+                copy.start()
+                copies.append(copy)
+            return copies
+
+        def send_coefficients(step, g, sends):
+            total = PART[step, :, share(g, me)]
+            for d in range(1, n_vel):
+                sends[d - 1].wait_recv()
+                total = total + GOT[step, g, d]
+            CO[step, :, share(g, me)] = shakhov_rows(total)
+            copies = []
+            for d in range(1, n_vel):
+                copy = pltpu.make_async_remote_copy(
+                    src_ref=CO.at[step, :, share(g, me)],
+                    dst_ref=CO.at[step, :, share(g, me)],
+                    send_sem=cs_sem.at[step, g, d],
+                    recv_sem=cr_sem.at[step, g, d],
+                    device_id={"vel": lax.rem(me + d, n_vel)},
+                    device_id_type=MESH,
+                )
+                copy.start()
+                copies.append(copy)
+            return copies
+
+        def ghost_copies(step, h, g):
+            copies = ghost_coefficients(step, h)
+            return [
+                copy
+                for k, copy in enumerate(copies)
+                if (depth - 1 - k if h == 1 else k) in groups[g]
+            ]
+
         stores = []
+
+        def relax_group(step, g, gathers):
+            for copy in gathers:
+                copy.wait_recv()
+            for h in range(2):
+                forwards = ghost_copies(step, h, g)
+                if forwards:
+                    @pl.when(has_down[h])
+                    def _(forwards=forwards):
+                        for copy in forwards:
+                            copy.start()
+            for n, x in enumerate(groups[g]):
+                load_coefficients(CO[step, :, place(x)], n % 2)
+                for h in range(2):
+                    q = q_of(h, x)
+                    relax(h, q, n % 2)
+                    if step + 1 == STEPS:
+                        copy = pltpu.make_async_copy(
+                            S.at[h, q], out.at[:, h, :, columns(x)], out_sem.at[h, x]
+                        )
+                        copy.start()
+                        stores.append(copy)
+
         for step in range(STEPS):
             last = step + 1 == STEPS
             if step == 0:
                 for copy in loads.values():
                     copy.wait()
-            transport([0, 1], G + 1, depth - 1)
-            for x in range(depth):
-                total = None
+            sends = {}
+            gathers = {}
+            split = len(groups) == 2
+            if split:
+                transport([0, 1], G + 1, depth - 2)
+                for x in groups[0]:
+                    first, second = moments(0, q_of(0, x)), moments(1, q_of(1, x))
+                    store_moments(step, x, [a + b for a, b in zip(first, second)])
+                sends[0] = send_moments(step, 0)
+                transport([0, 1], Q - 1, 1)
                 for h in range(2):
-                    q = x + G if h == 1 else depth - 1 + G - x
-                    if q > G:
-                        term = moments(h, q)
-                        total = term if total is None else [a + b for a, b in zip(total, term)]
-                for c, value in enumerate(total):
-                    start = x * section + c * wide
-                    PART[step, :, start : start + wide] = value
+                    store_moments(step, plane_of(h, Q - 1), moments(h, Q - 1))
+                if step == 0:
+                    gathers[0] = send_coefficients(step, 0, sends[0])
+                    relax_group(step, 0, gathers[0])
+            else:
+                transport([0, 1], G + 1, depth - 1)
+                for x in range(depth):
+                    total = None
+                    for h in range(2):
+                        if q_of(h, x) > G:
+                            term = moments(h, q_of(h, x))
+                            total = term if total is None else [a + b for a, b in zip(total, term)]
+                    store_moments(step, x, total)
 
             for h in range(2):
                 @pl.when(has_up[h])
@@ -361,14 +465,10 @@
                 @pl.when(has_up[h])
                 def _(h=h):
                     if step > 0:
-                        if step == 1:
-                            for copy in ghost_coefficients(0, h):
-                                copy.wait_recv()
-                        elif step - 1 < STEPS - 1:
-                            for copy in ghost_coefficients(step - 1, h):
-                                copy.wait_recv()
-                        for level in range(step):
-                            advance_ghost(h, G - step + level, level)
+                        for copy in ghost_coefficients(step - 1, h):
+                            copy.wait_recv()
+                    for level in range(step):
+                        advance_ghost(h, G - step + level, level)
 
                 @pl.when(jnp.logical_not(has_up[h]))
                 def _(h=h):
@@ -376,63 +476,18 @@
 
             transport([0, 1], G, 1)
             for h in range(2):
-                x = plane_of(h, G)
-                for c, value in enumerate(moments(h, G)):
-                    at = slice(x * section + c * wide, x * section + (c + 1) * wide)
-                    PART[step, :, at] = PART[step, :, at] + value
-
-            sends = []
-            for d in range(1, n_vel):
-                to = lax.rem(me + d, n_vel)
-                copy = pltpu.make_async_remote_copy(
-                    src_ref=PART.at[step, :, pl.ds(pl.multiple_of(to * piece, piece), piece)],
-                    dst_ref=GOT.at[step, d],
-                    send_sem=ps_sem.at[step, d],
-                    recv_sem=pr_sem.at[step, d],
-                    device_id={"vel": to},
-                    device_id_type=MESH,
-                )
-                copy.start()
-                sends.append(copy)
-            total = PART[step, :, own]
-            for d in range(1, n_vel):
-                sends[d - 1].wait_recv()
-                total = total + GOT[step, d]
-            CO[step, :, own] = shakhov_rows(total)
-            gathers = []
-            for d in range(1, n_vel):
-                to = lax.rem(me + d, n_vel)
-                copy = pltpu.make_async_remote_copy(
-                    src_ref=CO.at[step, :, own],
-                    dst_ref=CO.at[step, :, own],
-                    send_sem=cs_sem.at[step, d],
-                    recv_sem=cr_sem.at[step, d],
-                    device_id={"vel": to},
-                    device_id_type=MESH,
-                )
-                copy.start()
-                gathers.append(copy)
-            for copy in gathers:
-                copy.wait_recv()
-            if not last:
-                for h in range(2):
-                    @pl.when(has_down[h])
-                    def _(h=h):
-                        for copy in ghost_coefficients(step, h):
-                            copy.start()
-            for x in range(depth):
-                load_coefficients(CO[step, :, x * section : (x + 1) * section], x % 2)
-                for h in range(2):
-                    q = x + G if h == 1 else depth - 1 + G - x
-                    relax(h, q, x % 2)
-                    if last:
-                        copy = pltpu.make_async_copy(
-                            S.at[h, q], out.at[:, h, :, columns(x)], out_sem.at[h, x]
-                        )
-                        copy.start()
-                        stores.append(copy)
-            for copy in sends + gathers:
-                copy.wait_send()
+                add_moments(step, plane_of(h, G), moments(h, G))
+            rim = len(groups) - 1
+            sends[rim] = send_moments(step, rim)
+            for g in range(len(groups)):
+                if g not in gathers:
+                    gathers[g] = send_coefficients(step, g, sends[g])
+            for g in range(len(groups)):
+                if step > 0 or g == rim:
+                    relax_group(step, g, gathers[g])
+            for g in range(len(groups)):
+                for copy in sends[g] + gathers[g]:
+                    copy.wait_send()
             if not last:
                 for h in range(2):
                     @pl.when(has_down[h])
@@ -448,7 +503,7 @@
         pltpu.VMEM((2, Q, blocks, half, section), F32),
         pltpu.VMEM((2, Q, 8, section), F32),
         pltpu.VMEM((STEPS, FEATURES, cells), F32),
-        pltpu.VMEM((STEPS, n_vel, FEATURES, piece), F32),
+        pltpu.VMEM((STEPS, len(groups), n_vel, FEATURES, piece), F32),
         pltpu.VMEM((STEPS, COEFS, cells), F32),
         pltpu.VMEM((STEPS, 2, COEFS, (STEPS - 1) * section), F32),
         pltpu.VMEM((2, FEATURES, blocks * half), BF16),
@@ -464,10 +519,10 @@
         dma((2, depth)),
         dma((2, STEPS)),
         dma((2, STEPS)),
-        dma((STEPS, n_vel)),
-        dma((STEPS, n_vel)),
-        dma((STEPS, n_vel)),
-        dma((STEPS, n_vel)),
+        dma((STEPS, len(groups), n_vel)),
+        dma((STEPS, len(groups), n_vel)),
+        dma((STEPS, len(groups), n_vel)),
+        dma((STEPS, len(groups), n_vel)),
         dma((STEPS, 2, STEPS)),
         dma((STEPS, 2, STEPS)),
     ]
@@ -485,7 +540,7 @@
         blocks = rows // (2 * half)
         depth = cells // section
         kernel, scratch = make_kernel(n_vel, n_gx, blocks, half, depth, section, wall_mask.shape[0])
-        whole = pl.BlockSpec(memory_space=pl.ANY)
+        whole = pl.BlockSpec(memory_space=pltpu.HBM)
         out = pl.pallas_call(
             kernel,
             out_shape=jax.ShapeDtypeStruct((blocks, 2, half, cells), F32),

time: 68.3 us -> 65.7 us (0.962)
  Pallas kernels: 63.9 us -> 61.4 us
    pallas_call x1, Pallas kernels: 63.9 us -> 61.4 us  [per_device(): pl.pallas_call(kernel, out_shape=jax.ShapeDtypeStruct((blocks, 2, half, c...]
where the time goes in v3:
time: 65.7 us; the launch traced here: 65.5 us
  Pallas kernels  61.4 us (93%)
  local copies, waits for them, and re-layouts  4.14 us (6%)
    pallas_call x1, Pallas kernels, per_device(): pl.pallas_call(kernel, out_shape=jax.ShapeDtypeStruct((blocks, 2, half, c...  61.4 us
    unnamed x7, local copies, waits for them, and re-layouts  4.14 us

profile of v3, /device:TPU:17, one launch (start us, length us, event | category | flops | bytes accessed | tf_op | source)
XLA Modules:
  0.0 65.5 jit_solution(1225480809803918231)
XLA Ops:
  0.0 0.0 copy-start
  0.0 0.8 %copy-done = s32[16,512]{1,0:T(8,128)S(1)} copy-done((s32[16,512]{1,0:T(8,128)S(1)}, s32[16,512]{1,0:T(8,128)}, u32[]{:S(2)}) %copy-start) | copy-done | bytes 32792
  0.8 0.0 copy-start.1
  0.8 0.7 %copy-done.1 = s32[2,512]{1,0:T(2,128)S(1)} copy-done((s32[2,512]{1,0:T(2,128)S(1)}, s32[2,512]{1,0:T(2,128)}, u32[]{:S(2)}) %copy-start.1) | copy-done | bytes 4120
  1.4 0.0 copy-start.2
  1.4 0.7 %copy-done.2 = f32[512]{0:T(512)S(1)} copy-done((f32[512]{0:T(512)S(1)}, f32[512]{0:T(512)}, u32[]{:S(2)}) %copy-start.2) | copy-done | bytes 2072
  2.1 61.4 %shard_map.46 = f32[2,2,128,2048]{3,2,1,0:T(8,128)S(1)} custom-call(f32[2,2,128,2048]{3,2,1,0:T(8,128)} %bitcast.5, s32[16,512]{1,0:T(8,128)S(1)} %copy-done, s32[2,512]{1,0:T(2,128)S(1)} %copy-done.1, f32[4,128]{1,0:T(4,128)S(1)} %bitcast.4), custom_call_target="tpu_custom_call" | custom-call | tf_op jit(solution)/shard_map/pallas_call | solution.py:544
  63.5 2.0 %copy.6 = f32[512,2048]{1,0:T(8,128)} copy(f32[512,2048]{1,0:T(8,128)S(1)} %bitcast.3) | data formatting | bytes 8388608
Async XLA Ops:
  0.0 0.8 %copy-start = (s32[16,512]{1,0:T(8,128)S(1)}, s32[16,512]{1,0:T(8,128)}, u32[]{:S(2)}) copy-start(s32[16,512]{1,0:T(8,128)} %wall_in.1) | copy-start | bytes 98308
  0.8 0.7 %copy-start.1 = (s32[2,512]{1,0:T(2,128)S(1)}, s32[2,512]{1,0:T(2,128)}, u32[]{:S(2)}) copy-start(s32[2,512]{1,0:T(2,128)} %kind_in.1) | copy-start | bytes 12292
  1.4 0.7 %copy-start.2 = (f32[512]{0:T(512)S(1)}, f32[512]{0:T(512)}, u32[]{:S(2)}) copy-start(f32[512]{0:T(512)} %param.7) | copy-start | bytes 6148

commit v4 on v3

--- a/solution.py
+++ b/solution.py
@@ -324,7 +324,7 @@
             load_coefficients(CG[step, h, :, (G - 1 - q) * section : (G - q) * section], 0)
             relax(h, q, 0)
 
-        def ghost_coefficients(step, h):
+        def ghost_coefficients(step, h, sections=tuple(range(depth))):
             ghosts = STEPS - 1 - step
             if h == 1:
                 parts = [depth - 1 - k for k in range(ghosts)]
@@ -340,6 +340,7 @@
                     device_id_type=MESH,
                 )
                 for k, x in enumerate(parts)
+                if x in sections
             ]
 
         def share(g, who):
@@ -393,12 +394,7 @@
             return copies
 
         def ghost_copies(step, h, g):
-            copies = ghost_coefficients(step, h)
-            return [
-                copy
-                for k, copy in enumerate(copies)
-                if (depth - 1 - k if h == 1 else k) in groups[g]
-            ]
+            return ghost_coefficients(step, h, groups[g])
 
         stores = []
 
@@ -433,7 +429,8 @@
             gathers = {}
             split = len(groups) == 2
             if split:
-                transport([0, 1], G + 1, depth - 2)
+                early = depth - 3 if step == 0 else 0
+                transport([0, 1], G + 1, 1 + early)
                 for x in groups[0]:
                     first, second = moments(0, q_of(0, x)), moments(1, q_of(1, x))
                     store_moments(step, x, [a + b for a, b in zip(first, second)])
@@ -474,17 +471,19 @@
                 def _(h=h):
                     fill_edge(h)
 
+            if split and step > 0:
+                gathers[0] = send_coefficients(step, 0, sends[0])
             transport([0, 1], G, 1)
             for h in range(2):
                 add_moments(step, plane_of(h, G), moments(h, G))
             rim = len(groups) - 1
             sends[rim] = send_moments(step, rim)
-            for g in range(len(groups)):
-                if g not in gathers:
-                    gathers[g] = send_coefficients(step, g, sends[g])
-            for g in range(len(groups)):
-                if step > 0 or g == rim:
-                    relax_group(step, g, gathers[g])
+            if split and step > 0:
+                relax_group(step, 0, gathers[0])
+            gathers[rim] = send_coefficients(step, rim, sends[rim])
+            if split and not last:
+                transport([0, 1], G + 2, depth - 3)
+            relax_group(step, rim, gathers[rim])
             for g in range(len(groups)):
                 for copy in sends[g] + gathers[g]:
                     copy.wait_send()
@@ -548,7 +547,7 @@
             out_specs=whole,
             scratch_shapes=scratch,
             compiler_params=pltpu.CompilerParams(
-                collective_id=0, has_side_effects=True, vmem_limit_bytes=48 * 1024 * 1024
+                collective_id=0, has_side_effects=True, vmem_limit_bytes=64 * 1024 * 1024
             ),
         )(
             distribution.reshape(blocks, 2, half, cells),

time: 65.7 us -> 65.7 us (level)
  Pallas kernels: 61.4 us -> 60.7 us
    unnamed x7 -> x1, local copies, waits for them, and re-layouts: 4.14 us -> 4.7 us
where the time goes in v4:
time: 65.7 us; the launch traced here: 65.4 us
  Pallas kernels  60.7 us (92%)
  local copies, waits for them, and re-layouts  4.7 us (7%)
    pallas_call x1, Pallas kernels, per_device(): pl.pallas_call(kernel, out_shape=jax.ShapeDtypeStruct((blocks, 2, half, c...  60.7 us
    unnamed x1, local copies, waits for them, and re-layouts  4.7 us

profile of v4, /device:TPU:17, one launch (start us, length us, event | category | flops | bytes accessed | tf_op | source)
XLA Modules:
  0.0 65.4 jit_solution(15797575454856457174)
XLA Ops:
  0.0 60.7 %shard_map.46 = f32[2,2,128,2048]{3,2,1,0:T(8,128)} custom-call(f32[2,2,128,2048]{3,2,1,0:T(8,128)} %bitcast.4, s32[16,512]{1,0:T(8,128)} %wall_in.1, s32[2,512]{1,0:T(2,128)} %kind_in.1, f32[4,128]{1,0:T(4,128)} %bitcast.5), custom_call_target="tpu_custom_call" | custom-call | tf_op jit(solution)/shard_map/pallas_call | solution.py:543
  60.7 4.7 %copy.6 = f32[512,2048]{1,0:T(8,128)} copy(f32[512,2048]{1,0:T(8,128)} %bitcast.3) | data formatting | bytes 8388608

commit v5 on v4

--- a/solution.py
+++ b/solution.py
@@ -98,8 +98,8 @@
         return q - G if h == 1 else depth - 1 + G - q
 
     def kernel(
-        dist, wall_in, kind_in, inflow_in, out,
-        S, M, H, PART, GOT, CO, CG, PHI, L, RP, RS, INF, wall, kind, inflow, sm_sem,
+        dist, small, out,
+        S, M, H, PART, GOT, CO, CG, PHI, L, RP, RS, INF,
         in_sem, out_sem, hs_sem, hr_sem, ps_sem, pr_sem, cs_sem, cr_sem, gs_sem, gr_sem,
     ):
         me = lax.axis_index("vel")
@@ -128,12 +128,6 @@
                 )
                 copy.start()
                 loads[h, q] = copy
-
-        small = []
-        for k, (src, dst) in enumerate(((wall_in, wall), (kind_in, kind), (inflow_in, inflow))):
-            copy = pltpu.make_async_copy(src, dst, sm_sem.at[k])
-            copy.start()
-            small.append(copy)
 
         barrier = pltpu.get_barrier_semaphore()
         for d in range(1, n_vel):
@@ -172,21 +166,17 @@
 
         start_halo(0)
 
-        for copy in small:
-            copy.wait()
-
         first_iy = me * blocks
         lane = lax.broadcasted_iota(jnp.int32, (1, section), 1)
         y_at = lane // NZ
         z_at = lane % NZ
         vy_up = first_iy >= VS // 2
-        n_planes = wall.shape[0]
 
         def openness(x):
             at = pos * depth + x
-            row = wall[pl.ds(jnp.clip(at, 0, n_planes - 1), 1), :]
-            inside = jnp.logical_and(at >= 0, at < n_planes)
-            return jnp.where(inside, (1 - row).astype(F32), 1.0)
+            row = small[pl.ds(jnp.clip(at, 0, planes - 1), 1), :]
+            inside = jnp.logical_and(at >= 0, at < planes)
+            return jnp.where(inside, 1.0 - row, 1.0)
 
         for h in range(2):
             way = 1 if h == 1 else -1
@@ -221,7 +211,9 @@
             for b in range(blocks):
                 cy = jnp.full(shape, 2 * (first_iy + b) - (VS - 1), jnp.int32).astype(F32)
                 L[h, b] = features(index, cx, cy, cz).astype(BF16)
-                row = inflow[2 * b + h : 2 * b + h + 1, :]
+                start = (2 * b + h) * half
+                line = planes + 2 + start // section
+                row = small[line : line + 1, start % section : start % section + half]
                 INF[h, b] = jnp.broadcast_to(row, (half, half)).T
 
         lane_t = lax.broadcasted_iota(jnp.int32, (zh_rows, LANES), 1)
@@ -310,7 +302,7 @@
                 S[h, q, :, :, at] = (1.0 - relax_rate) * M[h, q, :, :, at] + fresh
 
         def fill_edge(h):
-            inner = kind[1 - h : 2 - h, :] == 1
+            inner = small[planes + 1 - h : planes + 2 - h, :] == 1.0
 
             for b in range(blocks):
                 for t in range(tiles):
@@ -435,6 +427,8 @@
                     first, second = moments(0, q_of(0, x)), moments(1, q_of(1, x))
                     store_moments(step, x, [a + b for a, b in zip(first, second)])
                 sends[0] = send_moments(step, 0)
+                if step > 0 and not last:
+                    start_halo(step + 1)
                 transport([0, 1], Q - 1, 1)
                 for h in range(2):
                     store_moments(step, plane_of(h, Q - 1), moments(h, Q - 1))
@@ -456,7 +450,7 @@
                 def _(h=h):
                     halo(h, step).wait_recv()
             finish_halo_send(step)
-            if not last:
+            if step == 0 or not (last or split):
                 start_halo(step + 1)
             for h in range(2):
                 @pl.when(has_up[h])
@@ -510,10 +504,6 @@
         pltpu.VMEM((2, FEATURES * TERMS, section), BF16),
         pltpu.VMEM((2, FEATURES * TERMS, section), BF16),
         pltpu.VMEM((2, blocks, half, half), F32),
-        pltpu.VMEM((planes, section), jnp.int32),
-        pltpu.VMEM((2, section), jnp.int32),
-        pltpu.VMEM((2 * blocks, half), F32),
-        dma((3,)),
         dma((2, depth)),
         dma((2, depth)),
         dma((2, STEPS)),
@@ -539,21 +529,23 @@
         blocks = rows // (2 * half)
         depth = cells // section
         kernel, scratch = make_kernel(n_vel, n_gx, blocks, half, depth, section, wall_mask.shape[0])
+        entering = jnp.pad(inflow, (0, -rows % section)).reshape(-1, section)
+        small = jnp.concatenate(
+            [wall_mask.astype(F32), boundary_kind.astype(F32), entering], axis=0
+        )
         whole = pl.BlockSpec(memory_space=pltpu.HBM)
         out = pl.pallas_call(
             kernel,
             out_shape=jax.ShapeDtypeStruct((blocks, 2, half, cells), F32),
-            in_specs=[whole] * 4,
+            in_specs=[whole, pl.BlockSpec(memory_space=pltpu.VMEM)],
             out_specs=whole,
             scratch_shapes=scratch,
             compiler_params=pltpu.CompilerParams(
-                collective_id=0, has_side_effects=True, vmem_limit_bytes=64 * 1024 * 1024
+                collective_id=0, has_side_effects=True, vmem_limit_bytes=48 * 1024 * 1024
             ),
         )(
             distribution.reshape(blocks, 2, half, cells),
-            wall_mask,
-            boundary_kind,
-            inflow.reshape(2 * blocks, half),
+            small,
         )
         return out.reshape(rows, cells)
 

time: 65.7 us -> 64.9 us (0.988)
  local copies, waits for them, and re-layouts: 4.7 us -> 2.02 us
  other arithmetic: 0 us -> 2.14 us
  Pallas kernels: 60.7 us -> 59.9 us
    unnamed x1, local copies, waits for them, and re-layouts: 4.7 us -> 2.02 us
    convert_element_type x0 -> x2, other arithmetic: none -> 1.45 us  [the longest x1 0.76 us: per_device(): wall_mask.astype(F32)]
    pallas_call x1, Pallas kernels: 60.7 us -> 59.9 us  [per_device(): pl.pallas_call(kernel, out_shape=jax.ShapeDtypeStruct((blocks, 2, half, c...]
    concatenate x0 -> x1, other arithmetic: none -> 0.69 us  [per_device(): jnp.concatenate([wall_mask.astype(F32), boundary_kind.astype(F32), enteri...]
where the time goes in v5:
time: 64.9 us; the launch traced here: 64.1 us
  Pallas kernels  59.9 us (92%)
  other arithmetic  2.14 us (3%)
  local copies, waits for them, and re-layouts  2.02 us (3%)
    pallas_call x1, Pallas kernels, per_device(): pl.pallas_call(kernel, out_shape=jax.ShapeDtypeStruct((blocks, 2, half, c...  59.9 us
    unnamed x1, local copies, waits for them, and re-layouts  2.02 us

profile of v5, /device:TPU:17, one launch (start us, length us, event | category | flops | bytes accessed | tf_op | source)
XLA Modules:
  0.0 64.1 jit_solution(2092992749433314496)
XLA Ops:
  0.0 0.7 %convert_element_type.7 = f32[2,512]{1,0:T(2,128)S(1)} convert(s32[2,512]{1,0:T(2,128)} %param.6) | non-fusion elementwise | flops 1024 | bytes 8192 | tf_op jit(solution)/shard_map/convert_element_type | solution.py:534
  0.7 0.8 %convert_element_type.6 = f32[16,512]{1,0:T(8,128)S(1)} convert(s32[16,512]{1,0:T(8,128)} %param.5) | non-fusion elementwise | flops 8192 | bytes 65536 | tf_op jit(solution)/shard_map/convert_element_type | solution.py:534
  1.5 0.7 %pad_maximum_fusion.small = f32[19,512]{1,0:T(8,128)S(1)} fusion(f32[1,512]{1,0:T(1,128)} %bitcast.5, f32[2,512]{1,0:T(2,128)S(1)} %convert_element_type.7, f32[16,512]{1,0:T(8,128)S(1)} %convert_element_type.6), kind=kLoop, calls=%fused_computation | loop fusion | flops 19456 | bytes 77824 | tf_op jit(solution)/shard_map/concatenate | solution.py:533
  2.1 59.9 %shard_map.46 = f32[2,2,128,2048]{3,2,1,0:T(8,128)S(1)} custom-call(f32[2,2,128,2048]{3,2,1,0:T(8,128)} %bitcast.4, f32[19,512]{1,0:T(8,128)S(1)} %pad_maximum_fusion.small), custom_call_target="tpu_custom_call" | custom-call | tf_op jit(solution)/shard_map/pallas_call | solution.py:537
  62.1 2.0 %copy.6 = f32[512,2048]{1,0:T(8,128)} copy(f32[512,2048]{1,0:T(8,128)S(1)} %bitcast.3) | data formatting | bytes 8388608
